TPU v7x, 32 devices: a whole 2x2x4 slice. The times are simulated.
32 devices in a mesh: dp: 8 (over z, y), seq: 4 (over x, core).
Axes of the slice: x: 2, y: 2, z: 4, core: 2. Of those that a mesh axis runs over, the one named last changes fastest.
Arguments:
- long_input: bfloat16 [8, 2048, 768], P('dp', 'seq'), may hold values from -6 to 6
- global_input: bfloat16 [8, 230, 768], P('dp'), may hold values from -6 to 6
- lengths: int32 [8], P('dp'), may hold values from 1024 to 2048, as said below
- w_query: bfloat16 [768, 768], replicated, may hold values from -0.21875 to 0.21875
- b_query: float32 [768], replicated, may hold values from -1.25 to 1.25
- w_key: bfloat16 [768, 768], replicated, may hold values from -0.21875 to 0.21875
- w_value: bfloat16 [768, 768], replicated, may hold values from -0.21875 to 0.21875
- b_value: float32 [768], replicated, may hold values from -1.25 to 1.25
- w_out: bfloat16 [768, 768], replicated, may hold values from -6 to 6
- b_out: float32 [768], replicated, may hold values from -1.25 to 1.25
- w_inner: bfloat16 [768, 3072], replicated, may hold values from -0.21875 to 0.21875
- b_inner: float32 [3072], replicated, may hold values from -1.25 to 1.25
- w_outer: bfloat16 [3072, 768], replicated, may hold values from -0.109375 to 0.109375
- b_outer: float32 [768], replicated, may hold values from -1.25 to 1.25
- norm1_gain: float32 [768], replicated, may hold values from 0.5 to 1.5
- norm1_shift: float32 [768], replicated, may hold values from -1.25 to 1.25
- norm2_gain: float32 [768], replicated, may hold values from 0.5 to 1.5
- norm2_shift: float32 [768], replicated, may hold values from -1.25 to 1.25
- rel_table: float32 [169, 12], replicated, may hold values from -6 to 6
- long_cotangent: bfloat16 [8, 2048, 768], P('dp', 'seq'), may hold values from -6 to 6
- global_cotangent: bfloat16 [8, 230, 768], P('dp'), may hold values from -6 to 6
Outputs:
- long_output: bfloat16 [8, 2048, 768], P('dp', 'seq')
- global_output: bfloat16 [8, 230, 768], P('dp')
- long_grad: float32 [8, 2048, 768], P('dp', 'seq')
- global_grad: float32 [8, 230, 768], P('dp')
- grad_w_query: float32 [768, 768], P(('dp', 'seq'))
- grad_b_query: float32 [768], P(('dp', 'seq'))
- grad_w_key: float32 [768, 768], P(('dp', 'seq'))
- grad_w_value: float32 [768, 768], P(('dp', 'seq'))
- grad_b_value: float32 [768], P(('dp', 'seq'))
- grad_w_out: float32 [768, 768], P(('dp', 'seq'))
- grad_b_out: float32 [768], P(('dp', 'seq'))
- grad_w_inner: float32 [768, 3072], P(('dp', 'seq'))
- grad_b_inner: float32 [3072], P(('dp', 'seq'))
- grad_w_outer: float32 [3072, 768], P(('dp', 'seq'))
- grad_b_outer: float32 [768], P(('dp', 'seq'))
- grad_norm1_gain: float32 [768], P(('dp', 'seq'))
- grad_norm1_shift: float32 [768], P(('dp', 'seq'))
- grad_norm2_gain: float32 [768], P(('dp', 'seq'))
- grad_norm2_shift: float32 [768], P(('dp', 'seq'))
- grad_rel_table: float32 [169, 12], replicated
Inputs may be any that keep to these rules, and one draw needn't show every extreme that they name: `lengths`: true long-token count of each document, whose long slots from it up to 2048 are padding; some document has all 2048 slots valid.
All inputs are finite; a program needn't handle non-finite values.
Results may differ from a plain program's by a relative error of at most 0.015.
Values may be sent and summed in bfloat16 or wider, within the bound.
A program may use at most 256 MiB of HBM per device.

v0:
```python
import functools
from typing import NamedTuple

import jax
import jax.numpy as jnp
from jax import lax
from jax.experimental import pallas as pl
from jax.experimental.pallas import tpu as pltpu
from jax.sharding import PartitionSpec as P

HD = 64
R = 84
PAIR = 2 * HD
HALO = 128
REACH = 96
GP = 256
SUB = 256
WINDOW = SUB + 2 * HALO
EPSILON = 1e-05
MASKED = -1e30
F32 = jnp.float32
BF16 = jnp.bfloat16


def norm_forward(values, gain, shift):
    average = jnp.mean(values, -1, keepdims=True)
    centred = values - average
    variance = jnp.mean(centred * centred, -1, keepdims=True)
    inverse = lax.rsqrt(variance + EPSILON)
    normed = centred * inverse
    return (normed * gain + shift, normed, inverse)


def norm_backward(grad_rows, normed, inverse, gain):
    scaled = grad_rows * gain
    grad_in = inverse * (
        scaled
        - jnp.mean(scaled, -1, keepdims=True)
        - normed * jnp.mean(scaled * normed, -1, keepdims=True)
    )
    return (grad_in, jnp.sum(grad_rows * normed, 0), jnp.sum(grad_rows, 0))


def smooth_gate(values):
    return jax.nn.gelu(values, approximate=True)


def dot_t(left, right):
    return lax.dot_general(left, right, (((1,), (1,)), ((), ())), preferred_element_type=F32)


def dot_n(left, right):
    return lax.dot_general(left, right, (((1,), (0,)), ((), ())), preferred_element_type=F32)


def t_dot(left, right):
    return lax.dot_general(left, right, (((0,), (0,)), ((), ())), preferred_element_type=F32)


def band_bias(table_row):
    spread = jnp.broadcast_to(table_row, (SUB, WINDOW))
    return pltpu.roll(spread, 0, 1, stride=1, stride_axis=0)


def diagonal_sums(rows):
    height, width = rows.shape
    while height > 8:
        height //= 2
        rows = rows[:height] + pltpu.roll(rows[height:], width - height, 1)
    row = lax.broadcasted_iota(jnp.int32, rows.shape, 0)
    for bit in (1, 2, 4):
        rows = jnp.where((row & bit) != 0, pltpu.roll(rows, width - bit, 1), rows)
    return jnp.sum(rows, 0, keepdims=True)


def lane_index():
    return lax.broadcasted_iota(jnp.int32, (1, PAIR), 1)


def own_half(head, value):
    low_lanes = lane_index() < HD
    return jnp.where(low_lanes if head == 0 else ~low_lanes, value, jnp.zeros_like(value))


def other_lane(head):
    return HD * (1 - head)


def with_lanes(head, value, columns):
    wide = own_half(head, value.astype(F32))
    lane = lane_index()
    for offset, column in enumerate(columns):
        wide = jnp.where(lane == other_lane(head) + offset, column, wide)
    return wide.astype(BF16)


def in_three(column):
    high = column.astype(BF16).astype(F32)
    middle = (column - high).astype(BF16).astype(F32)
    return (high, middle, column - high - middle)


def key_bias(first, rows, end):
    position = first + lax.broadcasted_iota(jnp.int32, (rows, 1), 0)
    return jnp.where((position >= 0) & (position < end), 0.0, MASKED)


def pick_column(rows, index):
    return jnp.sum(jnp.where(lane_index() == index, rows, 0.0), -1, keepdims=True)


def key_side(head, keys, bias):
    return with_lanes(head, keys, (bias, 1.0, 1.0, 1.0))


def value_side(head, values):
    return with_lanes(head, values, (1.0, 1.0, 1.0))


def softmax_rows(parts, value_parts, head):
    top = functools.reduce(
        jnp.maximum, [jnp.max(part, -1, keepdims=True) for part in parts]
    )
    mixed = sum(
        dot_n(jnp.exp(part - top).astype(BF16), values)
        for part, values in zip(parts, value_parts)
    )
    at = other_lane(head)
    total = mixed[:, at : at + 1]
    return mixed / total, top + jnp.log(total)


def seq_device(steps, seq_count):
    return (lax.axis_index("dp"), lax.rem(lax.axis_index("seq") + steps + seq_count, seq_count))


def row_norm(rows):
    centred = rows - jnp.mean(rows, -1, keepdims=True)
    inverse = lax.rsqrt(jnp.mean(centred * centred, -1, keepdims=True) + EPSILON)
    return centred * inverse, inverse


def put_column(ref, rows, index, column):
    ref[rows] = jnp.where(lane_index() == index, column, ref[rows])


def lanes_of(at):
    return pl.ds(pl.multiple_of(at * PAIR, PAIR), PAIR)


class Sizes(NamedTuple):
    block: int
    count: int
    quarter: int
    seq_count: int
    pairs: int


def attend_kernel(
    sizes,
    len_ref,
    tab_ref,
    long_ref,
    glob_ref,
    wq_ref,
    wk_ref,
    wv_ref,
    bq_ref,
    bv_ref,
    gain_ref,
    shift_ref,
    q_ref,
    kx_ref,
    vx_ref,
    kg_ref,
    vg_ref,
    o_ref,
    l_ref,
    lq_ref,
    part_o,
    part_l,
    from_o,
    from_l,
    halo_sends,
    halo_recvs,
    part_sends,
    part_recvs,
):
    block, count, quarter, seq_count, pairs = sizes
    ext = block + 2 * HALO
    seq_index = lax.axis_index("seq")
    scale = jnp.asarray(HD ** (-0.5), BF16)
    low_lanes = lane_index() < HD
    own_keys = slice(HALO, HALO + block)
    own_rows = pl.ds(pl.multiple_of(seq_index * quarter, quarter), quarter)
    neighbours = (seq_index > 0, seq_index < seq_count - 1)
    barrier = pltpu.get_barrier_semaphore()
    for step in range(1, seq_count):
        pl.semaphore_signal(
            barrier,
            inc=1,
            device_id=seq_device(step, seq_count),
            device_id_type=pl.DeviceIdType.MESH,
        )

    def halo_copies(direction):
        source = HALO if direction == 0 else HALO + block - REACH
        dest = HALO + block if direction == 0 else HALO - REACH
        for kind, ref in enumerate((kx_ref, vx_ref)):
            yield pltpu.make_async_remote_copy(
                src_ref=ref.at[source : source + REACH],
                dst_ref=ref.at[dest : dest + REACH],
                send_sem=halo_sends.at[direction, kind],
                recv_sem=halo_recvs.at[direction, kind],
                device_id=seq_device(2 * direction - 1, seq_count),
                device_id_type=pl.DeviceIdType.MESH,
            )

    def part_copies():
        for step in range(1, seq_count):
            device = seq_device(step, seq_count)
            rows = pl.ds(pl.multiple_of(device[1] * quarter, quarter), quarter)
            for kind, (source, dest) in enumerate(((part_o, from_o), (part_l, from_l))):
                yield step, kind, pltpu.make_async_remote_copy(
                    src_ref=source.at[rows],
                    dst_ref=dest.at[step - 1],
                    send_sem=part_sends.at[kind, step - 1],
                    recv_sem=part_recvs.at[kind, step - 1],
                    device_id=device,
                    device_id_type=pl.DeviceIdType.MESH,
                )

    gain, shift = gain_ref[...], shift_ref[...]
    normed_long = (row_norm(long_ref[...].astype(F32))[0] * gain + shift).astype(BF16)
    kx_ref[own_keys] = dot_n(normed_long, wk_ref[...]).astype(BF16)
    vx_ref[own_keys] = (dot_n(normed_long, wv_ref[...]) + bv_ref[...]).astype(BF16)
    pl.semaphore_wait(barrier, seq_count - 1)
    for direction, first in enumerate((HALO - REACH, HALO + block)):

        @pl.when(neighbours[direction])
        def _(direction=direction):
            for copy in halo_copies(direction):
                copy.start()

        outer = slice(0, first) if direction == 0 else slice(first + REACH, ext)
        for ref in (kx_ref, vx_ref):
            ref[outer] = jnp.zeros((HALO - REACH, ref.shape[1]), BF16)

        @pl.when(jnp.logical_not(neighbours[direction]))
        def _(first=first):
            for ref in (kx_ref, vx_ref):
                ref[first : first + REACH] = jnp.zeros((REACH, ref.shape[1]), BF16)

    normed_glob = (row_norm(glob_ref[...].astype(F32))[0] * gain + shift).astype(BF16)
    kg_ref[...] = dot_n(normed_glob, wk_ref[...]).astype(BF16)
    vg_ref[...] = (dot_n(normed_glob, wv_ref[...]) + bv_ref[...]).astype(BF16)
    q_ref[block:] = (dot_n(normed_glob, wq_ref[...]) + bq_ref[...]).astype(BF16)
    q_ref[:block] = (dot_n(normed_long, wq_ref[...]) + bq_ref[...]).astype(BF16)
    part_l[...] = jnp.zeros_like(part_l)
    l_ref[...] = jnp.zeros_like(l_ref)

    def glob_pair(pair, carry):
        lanes = lanes_of(pair)
        far_bias = key_bias(seq_index * block, block, len_ref[0])
        near_bias = key_bias(seq_index * quarter, quarter, count)
        query = q_ref[block:, lanes] * scale
        outs = []
        for head in range(2):
            q = with_lanes(head, query, (1.0,))
            far = dot_t(q, with_lanes(head, kx_ref[own_keys, lanes], (far_bias,)))
            near = dot_t(q, with_lanes(head, kg_ref[own_rows, lanes], (near_bias,)))
            out, norm = softmax_rows(
                [far, near],
                [
                    with_lanes(head, vx_ref[own_keys, lanes], (1.0,)),
                    with_lanes(head, vg_ref[own_rows, lanes], (1.0,)),
                ],
                head,
            )
            outs.append(out)
            put_column(part_l, slice(None), 2 * pair + head, norm)
        part_o[:, lanes] = jnp.where(low_lanes, outs[0], outs[1]).astype(BF16)
        return carry

    lax.fori_loop(0, pairs, glob_pair, 0)
    for _, _, copy in part_copies():
        copy.start()
    for direction in range(2):

        @pl.when(neighbours[1 - direction])
        def _(direction=direction):
            for copy in halo_copies(direction):
                copy.wait_recv()

    def long_pair(pair, carry):
        lanes = lanes_of(pair)
        long_bias = key_bias(seq_index * block - HALO, ext, len_ref[0])
        glob_bias = key_bias(0, GP, count)
        query = q_ref[:block, lanes] * scale
        outs = []
        for head in range(2):
            q = with_lanes(head, query, (1.0,))
            kx = with_lanes(head, kx_ref[:, lanes], (long_bias,))
            kg = with_lanes(head, kg_ref[:, lanes], (glob_bias,))
            vx, vg = (with_lanes(head, ref[:, lanes], (1.0,)) for ref in (vx_ref, vg_ref))
            bias = band_bias(tab_ref[pair, head : head + 1])
            mixed = []
            for start in range(0, block, SUB):
                rows, keys = slice(start, start + SUB), slice(start, start + WINDOW)
                out, norm = softmax_rows(
                    [dot_t(q[rows], kx[keys]) + bias, dot_t(q[rows], kg)], [vx[keys], vg], head
                )
                mixed.append(out)
                put_column(l_ref, rows, 2 * pair + head, norm)
            outs.append(jnp.concatenate(mixed, 0))
        o_ref[:block, lanes] = jnp.where(low_lanes, outs[0], outs[1]).astype(BF16)
        return carry

    lax.fori_loop(0, pairs, long_pair, 0)
    for _, _, copy in part_copies():
        copy.wait_recv()
    norms = [part_l[own_rows]] + [from_l[step] for step in range(seq_count - 1)]
    outs = [part_o[own_rows]] + [from_o[step] for step in range(seq_count - 1)]
    top = functools.reduce(jnp.maximum, norms)
    shares = [jnp.exp(norm - top) for norm in norms]
    total = sum(shares)
    lq_ref[...] = top + jnp.log(total)
    shares = [share / total for share in shares]
    for at in range(pairs):
        lanes = slice(at * PAIR, (at + 1) * PAIR)
        mixed = 0.0
        for share, out in zip(shares, outs):
            spread = jnp.where(
                low_lanes, share[:, 2 * at : 2 * at + 1], share[:, 2 * at + 1 : 2 * at + 2]
            )
            mixed += spread * out[:, lanes].astype(F32)
        o_ref[block:, lanes] = mixed.astype(BF16)
    for _, _, copy in part_copies():
        copy.wait_send()
    for direction in range(2):

        @pl.when(neighbours[direction])
        def _(direction=direction):
            for copy in halo_copies(direction):
                copy.wait_send()


def attend(sizes, doc_len, table, long_x, glob_x, *weights):
    block, count, quarter, seq_count, pairs = sizes
    width = long_x.shape[1]
    ext = block + 2 * HALO
    whole = pl.BlockSpec(memory_space=pltpu.VMEM)
    shape = jax.ShapeDtypeStruct
    others = seq_count - 1
    return pl.pallas_call(
        functools.partial(attend_kernel, sizes),
        in_specs=[pl.BlockSpec(memory_space=pltpu.SMEM)] + [whole] * 10,
        out_specs=[whole] * 8,
        out_shape=[
            shape((block + GP, width), BF16),
            shape((ext, width), BF16),
            shape((ext, width), BF16),
            shape((GP, width), BF16),
            shape((GP, width), BF16),
            shape((block + quarter, width), BF16),
            shape((block, PAIR), F32),
            shape((quarter, PAIR), F32),
        ],
        scratch_shapes=[
            pltpu.VMEM((GP, width), BF16),
            pltpu.VMEM((GP, PAIR), F32),
            pltpu.VMEM((others, quarter, width), BF16),
            pltpu.VMEM((others, quarter, PAIR), F32),
            pltpu.SemaphoreType.DMA((2, 2)),
            pltpu.SemaphoreType.DMA((2, 2)),
            pltpu.SemaphoreType.DMA((2, others)),
            pltpu.SemaphoreType.DMA((2, others)),
        ],
        compiler_params=pltpu.CompilerParams(
            collective_id=3, has_side_effects=True, vmem_limit_bytes=56 * 2**20
        ),
        name="attend",
    )(doc_len, table, long_x, glob_x, *weights)


class Reducer:
    def __init__(self, mesh_ids, rows, pieces, mine, from_core, from_one, from_two, from_z, sems):
        self.ids = mesh_ids
        half = (rows // 2 + 15) // 16 * 16
        self.halves = (slice(0, half), slice(half, rows))
        self.pieces, self.mine = pieces, mine
        self.from_core, self.from_one, self.from_two, self.from_z = (
            from_core,
            from_one,
            from_two,
            from_z,
        )
        self.local, self.sends, self.recvs = sems

    @staticmethod
    def scratch(rows, width):
        half = (rows // 2 + 15) // 16 * 16
        return [
            pltpu.VMEM((4, 2, 2, rows, width), BF16),
            pltpu.VMEM((4, 2, 2, rows, width), BF16),
            pltpu.VMEM((4, 2, rows, width), BF16),
            pltpu.VMEM((4, rows, width), BF16),
            pltpu.VMEM((3, rows, width), BF16),
            pltpu.SemaphoreType.DMA((4,)),
            pltpu.SemaphoreType.DMA((6, 4)),
            pltpu.SemaphoreType.DMA((6, 4)),
        ]

    def partners(self):
        z, y, x, core = self.ids
        dp, seq = z * 2 + y, x * 2 + core
        near = [(dp, x * 2 + 1 - core), (dp, (1 - x) * 2 + core), (z * 2 + 1 - y, seq)]
        return near + [(lax.rem(z + step, 4) * 2 + y, seq) for step in (1, 2, 3)]

    def target(self, chunk):
        return lax.rem(self.ids[0] + 1 + chunk, 4)

    def remote(self, source, dest, kind, chunk, partner):
        return pltpu.make_async_remote_copy(
            src_ref=source,
            dst_ref=dest,
            send_sem=self.sends.at[kind, chunk],
            recv_sem=self.recvs.at[kind, chunk],
            device_id=self.partners()[partner],
            device_id_type=pl.DeviceIdType.MESH,
        )

    def own_copy(self, chunk):
        z, y, x, core = self.ids
        to = self.target(chunk)
        return pltpu.make_async_copy(
            self.pieces.at[core, to], self.mine.at[to], self.local.at[chunk]
        )

    def core_copy(self, chunk):
        z, y, x, core = self.ids
        to = self.target(chunk)
        return self.remote(self.pieces.at[1 - core, to], self.from_core.at[to], 0, chunk, 0)

    def first_copies(self, chunk):
        z, y, x, core = self.ids
        to = self.target(chunk)
        one, two = self.halves
        return (
            self.remote(
                self.mine.at[to, :, 1 - x, one], self.from_one.at[to, :, one], 1, chunk, 1
            ),
            self.remote(
                self.mine.at[to, 1 - y, :, two], self.from_one.at[to, :, two], 2, chunk, 2
            ),
        )

    def second_copies(self, chunk):
        z, y, x, core = self.ids
        to = self.target(chunk)
        one, two = self.halves
        return (
            self.remote(
                self.mine.at[to, 1 - y, x, one], self.from_two.at[to, one], 3, chunk, 2
            ),
            self.remote(
                self.mine.at[to, y, 1 - x, two], self.from_two.at[to, two], 4, chunk, 1
            ),
        )

    def last_copy(self, chunk):
        z, y, x, core = self.ids
        return self.remote(
            self.mine.at[self.target(chunk), y, x], self.from_z.at[chunk], 5, chunk, 3 + chunk
        )

    def start(self):
        for chunk in range(4):
            self.core_copy(chunk).start()
            self.own_copy(chunk).start()

    def add_core(self, chunk):
        to = self.target(chunk)
        self.own_copy(chunk).wait()
        self.core_copy(chunk).wait_recv()

        def add(index, carry):
            at = (to, lax.div(index, 2), lax.rem(index, 2))
            self.mine[at] = (self.mine[at].astype(F32) + self.from_core[at].astype(F32)).astype(
                BF16
            )
            return carry

        lax.fori_loop(0, 4, add, 0)
        for copy in self.first_copies(chunk):
            copy.start()

    def add_first(self, chunk):
        z, y, x, core = self.ids
        one, two = self.halves
        to = self.target(chunk)
        for copy in self.first_copies(chunk):
            copy.wait_recv()

        def add(index, carry):
            for at, rows in (((to, index, x), one), ((to, y, index), two)):
                self.mine[at + (rows,)] = (
                    self.mine[at + (rows,)].astype(F32)
                    + self.from_one[to, index, rows].astype(F32)
                ).astype(BF16)
            return carry

        lax.fori_loop(0, 2, add, 0)
        for copy in self.second_copies(chunk):
            copy.start()

    def add_second(self, chunk):
        z, y, x, core = self.ids
        to = self.target(chunk)
        for copy in self.second_copies(chunk):
            copy.wait_recv()
        if chunk < 3:
            self.mine[to, y, x] = (
                self.mine[to, y, x].astype(F32) + self.from_two[to].astype(F32)
            ).astype(BF16)
            self.last_copy(chunk).start()

    def finish(self, out):
        z, y, x, core = self.ids
        total = self.mine[z, y, x].astype(F32) + self.from_two[z].astype(F32)
        for chunk in range(3):
            self.last_copy(chunk).wait_recv()
            total += self.from_z[chunk].astype(F32)
        out[...] = total
        for chunk in range(4):
            self.core_copy(chunk).wait_send()
            for copy in self.first_copies(chunk) + self.second_copies(chunk):
                copy.wait_send()
            if chunk < 3:
                self.last_copy(chunk).wait_send()


def mesh_ids():
    dp, seq = lax.axis_index("dp"), lax.axis_index("seq")
    return lax.div(dp, 2), lax.rem(dp, 2), lax.div(seq, 2), lax.rem(seq, 2)


def meet(devices):
    barrier = pltpu.get_barrier_semaphore()
    for device in devices:
        pl.semaphore_signal(barrier, inc=1, device_id=device, device_id_type=pl.DeviceIdType.MESH)
    pl.semaphore_wait(barrier, len(devices))


EARLY_PLAN = (
    (1, "add_core", 0),
    (2, "add_core", 1),
    (3, "add_core", 2),
    (4, "add_core", 3),
    (5, "add_first", 0),
    (8, "add_first", 1),
    (9, "add_second", 0),
    (11, "add_first", 2),
    (11, "add_second", 1),
    (11, "add_first", 3),
    (11, "add_second", 2),
    (11, "add_second", 3),
)
LATE_PLAN = (
    ("add_core", 0),
    ("add_core", 1),
    ("add_first", 0),
    ("add_core", 2),
    ("add_first", 1),
    ("add_second", 0),
    ("add_core", 3),
    ("add_first", 2),
    ("add_second", 1),
    ("add_first", 3),
    ("add_second", 2),
    ("add_second", 3),
)


def late_kernel(rows, pieces_ref, table_ref, out_ref, total_ref, *scratch):
    reducer = Reducer(mesh_ids(), rows, pieces_ref, *scratch[:5], scratch[5:8])
    kept, arrived, sends, recvs = scratch[8:]
    z, y, x, core = mesh_ids()
    dp, seq = lax.axis_index("dp"), lax.axis_index("seq")
    flip_low = z + 1 - 2 * lax.rem(z, 2)
    flip_high = lax.rem(z + 2, 4)
    partners = (
        (dp, x * 2 + 1 - core),
        (dp, (1 - x) * 2 + core),
        (z * 2 + 1 - y, seq),
        (flip_low * 2 + y, seq),
        (flip_high * 2 + y, seq),
    )

    def table_copy(stage):
        return pltpu.make_async_remote_copy(
            src_ref=kept.at[stage],
            dst_ref=arrived.at[stage],
            send_sem=sends.at[stage],
            recv_sem=recvs.at[stage],
            device_id=partners[stage],
            device_id_type=pl.DeviceIdType.MESH,
        )

    meet(reducer.partners())
    reducer.start()
    kept[0] = table_ref[...]
    table_copy(0).start()
    for number, (act, chunk) in enumerate(LATE_PLAN):
        getattr(reducer, act)(chunk)
        if number % 2 == 1:
            stage = number // 2
            if stage < 5:
                table_copy(stage).wait_recv()
                kept[stage + 1] = kept[stage] + arrived[stage]
            if stage < 4:
                table_copy(stage + 1).start()
    total_ref[...] = kept[5]
    reducer.finish(out_ref)
    for stage in range(5):
        table_copy(stage).wait_send()


def reduce_late(pieces, table):
    rows, width = pieces.shape[-2:]
    whole = pl.BlockSpec(memory_space=pltpu.VMEM)
    return pl.pallas_call(
        functools.partial(late_kernel, rows),
        in_specs=[pl.BlockSpec(memory_space=pl.ANY), whole],
        out_specs=[whole, whole],
        out_shape=[
            jax.ShapeDtypeStruct((rows, width), F32),
            jax.ShapeDtypeStruct(table.shape, F32),
        ],
        scratch_shapes=Reducer.scratch(rows, width)
        + [
            pltpu.VMEM((6,) + table.shape, F32),
            pltpu.VMEM((5,) + table.shape, F32),
            pltpu.SemaphoreType.DMA((5,)),
            pltpu.SemaphoreType.DMA((5,)),
        ],
        compiler_params=pltpu.CompilerParams(
            collective_id=2, has_side_effects=True, vmem_limit_bytes=40 * 2**20
        ),
        name="reduce_late",
    )(pieces, table)


def has_plan():
    return (lax.axis_size("dp"), lax.axis_size("seq")) == (8, 4)


def by_core(parts):
    return parts.astype(BF16).reshape((4, 2, 2, 2) + parts.shape[1:]).transpose(3, 0, 1, 2, 4, 5)


def scattered(parts):
    return lax.psum_scatter(
        parts.astype(BF16), ("dp", "seq"), scatter_dimension=0, tiled=True
    )[0].astype(F32)


class BackSizes(NamedTuple):
    block: int
    count: int
    quarter: int
    seq_count: int
    pairs: int
    early_rows: int


def back_kernel(
    sizes,
    len_ref,
    tab_ref,
    q_ref,
    kx_ref,
    vx_ref,
    kg_ref,
    vg_ref,
    o_ref,
    do_ref,
    l_ref,
    doq_ref,
    ldq_ref,
    *rest,
):
    block, count, quarter, seq_count, pairs, early_rows = sizes
    reduces = early_rows > 0
    if reduces:
        pieces_ref, rest = rest[0], rest[1:]
    dq_ref, dk_ref, dv_ref, dtab_ref, *rest = rest
    if reduces:
        early_ref, rest = rest[0], rest[1:]
    (
        dkx,
        dvx,
        dkg,
        dvg,
        glob_send,
        glob_recv,
        halo_send,
        halo_recv,
        dog_all,
        ld_all,
        every_sends,
        every_recvs,
        glob_sends,
        glob_recvs,
        halo_sends,
        halo_recvs,
        *rest,
    ) = rest
    number = pl.program_id(0)
    pair = lax.rem(number, pairs)
    seq_index = lax.axis_index("seq")
    reducer = Reducer(mesh_ids(), early_rows, pieces_ref, *rest[:5], rest[5:]) if reduces else None
    scale = HD ** (-0.5)
    low_lanes = lane_index() < HD
    own_keys = slice(HALO, HALO + block)
    own_rows = pl.ds(pl.multiple_of(seq_index * quarter, quarter), quarter)

    def every_copies():
        for step in range(1, seq_count):
            for kind, (source, dest) in enumerate(((doq_ref, dog_all), (ldq_ref, ld_all))):
                yield pltpu.make_async_remote_copy(
                    src_ref=source,
                    dst_ref=dest.at[seq_index],
                    send_sem=every_sends.at[kind, step - 1],
                    recv_sem=every_recvs.at[kind, step - 1],
                    device_id=seq_device(step, seq_count),
                    device_id_type=pl.DeviceIdType.MESH,
                )

    def glob_copies(at):
        for step in range(1, seq_count):
            device = seq_device(step, seq_count)
            yield pltpu.make_async_remote_copy(
                src_ref=glob_send.at[device[1], at],
                dst_ref=glob_recv.at[step - 1, at],
                send_sem=glob_sends.at[step - 1, at],
                recv_sem=glob_recvs.at[step - 1, at],
                device_id=device,
                device_id_type=pl.DeviceIdType.MESH,
            )

    def halo_copy(direction):
        return pltpu.make_async_remote_copy(
            src_ref=halo_send.at[direction],
            dst_ref=halo_recv.at[direction],
            send_sem=halo_sends.at[direction],
            recv_sem=halo_recvs.at[direction],
            device_id=seq_device(2 * direction - 1, seq_count),
            device_id_type=pl.DeviceIdType.MESH,
        )

    has_low, has_high = seq_index > 0, seq_index < seq_count - 1
    sends_to = (has_low, has_high)
    gets_from = (has_high, has_low)

    @pl.when(number == 0)
    def _():
        others = [seq_device(step, seq_count) for step in range(1, seq_count)]
        meet(others + (reducer.partners()[2:] if reduces else []))
        for copy in every_copies():
            copy.start()
        if reduces:
            reducer.start()
        dog_all[seq_index] = doq_ref[...]
        ld_all[seq_index] = ldq_ref[...]

    if reduces:
        for at, act, chunk in EARLY_PLAN:

            @pl.when(number == at)
            def _(act=act, chunk=chunk):
                getattr(reducer, act)(chunk)

    @pl.when(number < pairs)
    def _():
        long_bias = key_bias(seq_index * block - HALO, block + 2 * HALO, len_ref[0])
        glob_bias = key_bias(0, GP, count)
        query = q_ref[:block] * jnp.asarray(scale, BF16)
        grad_o = do_ref[...]
        both = grad_o.astype(F32) * o_ref[...].astype(F32)
        heads = []
        for head in range(2):
            norm = in_three(-pick_column(l_ref[...], 2 * pair + head))
            delta = in_three(-jnp.sum(own_half(head, both), -1, keepdims=True))
            heads.append(
                dict(
                    q=own_half(head, query),
                    do=own_half(head, grad_o),
                    qa=with_lanes(head, query, (1.0,) + norm),
                    doa=with_lanes(head, grad_o, delta),
                    kxa=key_side(head, kx_ref[...], long_bias),
                    vxa=value_side(head, vx_ref[...]),
                    kga=key_side(head, kg_ref[...], glob_bias),
                    vga=value_side(head, vg_ref[...]),
                    bias=band_bias(tab_ref[0, head : head + 1]),
                )
            )
        dkx[pair] = jnp.zeros_like(dkx[pair])
        dvx[pair] = jnp.zeros_like(dvx[pair])
        table_sums = [0.0, 0.0]
        grads_q = []
        for start in range(0, block, SUB):
            rows, keys = slice(start, start + SUB), slice(start, start + WINDOW)
            outs, probs, grads = [], [], []
            for head, own in enumerate(heads):
                band = jnp.exp(dot_t(own["qa"][rows], own["kxa"][keys]) + own["bias"])
                band_ds = band * dot_t(own["doa"][rows], own["vxa"][keys])
                table_sums[head] += band_ds
                glob = jnp.exp(dot_t(own["qa"][rows], own["kga"]))
                glob_ds = (glob * dot_t(own["doa"][rows], own["vga"])).astype(BF16)
                band_ds = band_ds.astype(BF16)
                outs.append(dot_n(band_ds, kx_ref[keys]) + dot_n(glob_ds, kg_ref[...]))
                probs.append((band.astype(BF16), glob.astype(BF16)))
                grads.append((band_ds, glob_ds))
            grads_q.append(jnp.where(low_lanes, outs[0], outs[1]))
            own_q = jnp.concatenate([own["q"][rows] for own in heads], 0)
            own_do = jnp.concatenate([own["do"][rows] for own in heads], 0)
            band, glob = (jnp.concatenate(part, 0) for part in zip(*probs))
            band_ds, glob_ds = (jnp.concatenate(part, 0) for part in zip(*grads))
            dkx[pair, keys] += t_dot(band_ds, own_q)
            dvx[pair, keys] += t_dot(band, own_do)
            more_k, more_v = t_dot(glob_ds, own_q), t_dot(glob, own_do)
            dkg[pair] = more_k if start == 0 else dkg[pair] + more_k
            dvg[pair] = more_v if start == 0 else dvg[pair] + more_v
        dq_ref[:block, lanes_of(pair)] = (jnp.concatenate(grads_q, 0) * scale).astype(BF16)
        for head in range(2):
            dtab_ref[pair, head : head + 1] = diagonal_sums(table_sums[head])

    @pl.when(number == pairs)
    def _():
        for kind, total in enumerate((dkx, dvx)):
            for direction, first in enumerate((HALO - REACH, HALO + block)):
                halo_send[direction, kind] = total[:, first : first + REACH].astype(BF16)
        for direction in range(2):

            @pl.when(sends_to[direction])
            def _(direction=direction):
                halo_copy(direction).start()

        for copy in every_copies():
            copy.wait_recv()

    @pl.when(number >= pairs)
    def _():
        long_bias = key_bias(seq_index * block, block, len_ref[0])
        near_bias = key_bias(seq_index * quarter, quarter, count)
        query = q_ref[block:] * jnp.asarray(scale, BF16)
        grad_o = dog_all[:, :, lanes_of(pair)].reshape(GP, PAIR)
        stats = ld_all[...].reshape(GP, PAIR)
        far_k, far_v = kx_ref[own_keys], vx_ref[own_keys]
        near_k, near_v = kg_ref[own_rows], vg_ref[own_rows]
        outs, kept = [], []
        for head in range(2):
            norm = in_three(-pick_column(stats, 2 * pair + head))
            delta = in_three(-pick_column(stats, HD + 2 * pair + head))
            qa = with_lanes(head, query, (1.0,) + norm)
            doa = with_lanes(head, grad_o, delta)
            far = jnp.exp(dot_t(qa, key_side(head, far_k, long_bias)))
            near = jnp.exp(dot_t(qa, key_side(head, near_k, near_bias)))
            far_ds = (far * dot_t(doa, value_side(head, far_v))).astype(BF16)
            near_ds = (near * dot_t(doa, value_side(head, near_v))).astype(BF16)
            outs.append(dot_n(far_ds, far_k) + dot_n(near_ds, near_k))
            kept.append(
                (
                    own_half(head, query),
                    own_half(head, grad_o),
                    far.astype(BF16),
                    near.astype(BF16),
                    far_ds,
                    near_ds,
                )
            )
        own_q, own_do, far, near, far_ds, near_ds = (
            jnp.concatenate(part, 0) for part in zip(*kept)
        )
        dkx[pair, own_keys] += t_dot(far_ds, own_q)
        dvx[pair, own_keys] += t_dot(far, own_do)
        dkg[pair, own_rows] += t_dot(near_ds, own_q)
        dvg[pair, own_rows] += t_dot(near, own_do)
        glob_dq = jnp.where(low_lanes, outs[0], outs[1]) * scale
        for at, grad in enumerate((glob_dq, dkg[pair], dvg[pair])):
            glob_send[:, pair, :, at * PAIR : (at + 1) * PAIR] = grad.astype(BF16).reshape(
                seq_count, quarter, PAIR
            )
        for copy in glob_copies(pair):
            copy.start()

    @pl.when(number == 2 * pairs - 1)
    def _():
        for direction in range(2):

            @pl.when(gets_from[direction])
            def _(direction=direction):
                halo_copy(direction).wait_recv()

            @pl.when(jnp.logical_not(gets_from[direction]))
            def _(direction=direction):
                halo_recv[direction] = jnp.zeros_like(halo_recv[direction])

        for at in range(pairs):
            lanes = slice(at * PAIR, (at + 1) * PAIR)
            for kind, (total, out) in enumerate(((dkx, dk_ref), (dvx, dv_ref))):
                first, last = HALO + REACH, HALO + block - REACH
                out[:REACH, lanes] = (
                    total[at, HALO:first] + halo_recv[1, kind, at].astype(F32)
                ).astype(BF16)
                out[REACH : block - REACH, lanes] = total[at, first:last].astype(BF16)
                out[block - REACH : block, lanes] = (
                    total[at, last : HALO + block] + halo_recv[0, kind, at].astype(F32)
                ).astype(BF16)
        for at in range(pairs):
            lanes = slice(at * PAIR, (at + 1) * PAIR)
            total = glob_send[seq_index, at].astype(F32)
            for step, copy in enumerate(glob_copies(at)):
                copy.wait_recv()
                total += glob_recv[step, at].astype(F32)
            for kind, out in enumerate((dq_ref, dk_ref, dv_ref)):
                out[block:, lanes] = total[:, kind * PAIR : (kind + 1) * PAIR].astype(BF16)
        for at in range(pairs):
            for copy in glob_copies(at):
                copy.wait_send()
        for copy in every_copies():
            copy.wait_send()
        for direction in range(2):

            @pl.when(sends_to[direction])
            def _(direction=direction):
                halo_copy(direction).wait_send()

        if reduces:
            reducer.finish(early_ref)


def attend_back(sizes, doc_len, table, q, kx, vx, kg, vg, o, do, l, doq, ldq, pieces=None):
    block, count, quarter, seq_count, pairs, early_rows = sizes
    width = q.shape[1]
    ext = block + 2 * HALO
    cols = lambda rows: pl.BlockSpec((rows, PAIR), lambda i: (0, lax.rem(i, pairs)))
    whole = pl.BlockSpec(memory_space=pltpu.VMEM)
    shape = jax.ShapeDtypeStruct
    in_specs = [
        pl.BlockSpec(memory_space=pltpu.SMEM),
        pl.BlockSpec((1, 2, WINDOW), lambda i: (lax.rem(i, pairs), 0, 0)),
        cols(block + GP),
        cols(ext),
        cols(ext),
        cols(GP),
        cols(GP),
        cols(block),
        cols(block),
        whole,
        whole,
        whole,
    ]
    rows = block + quarter
    outs = [shape((rows, width), BF16)] * 3 + [shape((pairs, 2, WINDOW), F32)]
    others = seq_count - 1
    scratch = [
        pltpu.VMEM((pairs, ext, PAIR), F32),
        pltpu.VMEM((pairs, ext, PAIR), F32),
        pltpu.VMEM((pairs, GP, PAIR), F32),
        pltpu.VMEM((pairs, GP, PAIR), F32),
        pltpu.VMEM((seq_count, pairs, quarter, 3 * PAIR), BF16),
        pltpu.VMEM((others, pairs, quarter, 3 * PAIR), BF16),
        pltpu.VMEM((2, 2, pairs, REACH, PAIR), BF16),
        pltpu.VMEM((2, 2, pairs, REACH, PAIR), BF16),
        pltpu.VMEM((seq_count, quarter, width), BF16),
        pltpu.VMEM((seq_count, quarter, PAIR), F32),
        pltpu.SemaphoreType.DMA((2, others)),
        pltpu.SemaphoreType.DMA((2, others)),
        pltpu.SemaphoreType.DMA((others, pairs)),
        pltpu.SemaphoreType.DMA((others, pairs)),
        pltpu.SemaphoreType.DMA((2,)),
        pltpu.SemaphoreType.DMA((2,)),
    ]
    args = [doc_len, table, q, kx, vx, kg, vg, o, do, l, doq, ldq]
    if early_rows:
        in_specs.append(pl.BlockSpec(memory_space=pl.ANY))
        outs.append(shape((early_rows, width), F32))
        scratch += Reducer.scratch(early_rows, width)
        args.append(pieces)
    return pl.pallas_call(
        functools.partial(back_kernel, sizes),
        grid=(2 * pairs,),
        in_specs=in_specs,
        out_specs=[whole] * len(outs),
        out_shape=outs,
        scratch_shapes=scratch,
        compiler_params=pltpu.CompilerParams(
            collective_id=1, has_side_effects=True, vmem_limit_bytes=60 * 2**20
        ),
        name="attend_back",
    )(*args)


def matmul(left, right):
    return jnp.dot(left, right, preferred_element_type=F32)


def rows_dot(left, right):
    return jnp.einsum("rd,re->de", left, right, preferred_element_type=F32)


def back_dot(left, right):
    return lax.dot_general(left, right, (((1,), (1,)), ((), ())), preferred_element_type=F32)


def on_device(
    long_input,
    global_input,
    lengths,
    w_query,
    b_query,
    w_key,
    w_value,
    b_value,
    w_out,
    b_out,
    w_inner,
    b_inner,
    w_outer,
    b_outer,
    norm1_gain,
    norm1_shift,
    norm2_gain,
    norm2_shift,
    rel_table,
    long_cotangent,
    global_cotangent,
):
    seq_count = lax.axis_size("seq")
    data_count = lax.axis_size("dp")
    seq_index = lax.axis_index("seq")
    block = long_input.shape[1]
    count = global_input.shape[1]
    width = long_input.shape[2]
    heads = rel_table.shape[1]
    pairs = heads // 2
    labels = 2 * R + 1
    quarter = GP // seq_count
    sizes = Sizes(block, count, quarter, seq_count, pairs)
    row_valid = (seq_index * block + jnp.arange(block, dtype=jnp.int32)) < lengths[0]
    table = jnp.pad(
        rel_table.T,
        ((0, 0), (HALO - R, WINDOW - labels - HALO + R)),
        constant_values=MASKED,
    ).reshape(pairs, 2, WINDOW)

    glob_x = jnp.pad(global_input[0], ((0, GP - count), (0, 0)))
    glob_dy = jnp.pad(global_cotangent[0], ((0, GP - count), (0, 0)))
    own_glob = lambda a: lax.dynamic_slice_in_dim(a, seq_index * quarter, quarter, 0)
    own_x = jnp.concatenate([long_input[0], own_glob(glob_x)], 0).astype(F32)
    queries, kx, vx, kg, vg, attn_low, long_l, glob_l = attend(
        sizes,
        lengths,
        table,
        long_input[0],
        glob_x,
        w_query,
        w_key,
        w_value,
        b_query[None],
        b_value[None],
        norm1_gain[None],
        norm1_shift[None],
    )

    residual_mid = own_x + matmul(attn_low, w_out) + b_out
    normed_two, hat_two, inv_two = norm_forward(residual_mid, norm2_gain, norm2_shift)
    normed_two_low = normed_two.astype(BF16)
    hidden_pre = matmul(normed_two_low, w_inner) + b_inner
    activated, gelu_back = jax.vjp(smooth_gate, hidden_pre)
    activated_low = activated.astype(BF16)
    result = residual_mid + matmul(activated_low, w_outer) + b_outer
    long_result = jnp.where(row_valid[:, None], result[:block], 0.0).astype(BF16)
    grad_y_low = jnp.concatenate(
        [
            jnp.where(row_valid[:, None], long_cotangent[0], jnp.zeros_like(long_cotangent[0])),
            own_glob(glob_dy),
        ],
        0,
    )
    grad_y = grad_y_low.astype(F32)
    grad_b_outer = jnp.sum(grad_y, 0)
    grad_w_outer = rows_dot(activated_low, grad_y_low)
    (grad_hidden,) = gelu_back(back_dot(grad_y_low, w_outer))
    grad_b_inner = jnp.sum(grad_hidden, 0)
    hidden_low = grad_hidden.astype(BF16)
    grad_w_inner = rows_dot(normed_two_low, hidden_low)
    grad_from_two, grad_gain_two, grad_shift_two = norm_backward(
        back_dot(hidden_low, w_inner), hat_two, inv_two, norm2_gain
    )
    grad_mid = grad_y + grad_from_two
    grad_b_out = jnp.sum(grad_mid, 0)
    grad_mid_low = grad_mid.astype(BF16)
    grad_w_out = rows_dot(attn_low, grad_mid_low)
    grad_attn = back_dot(grad_mid_low, w_out).astype(BF16)

    glob_do = grad_attn[block:]
    glob_o = attn_low[block:].astype(F32)
    glob_delta = jnp.sum((glob_do.astype(F32) * glob_o).reshape(quarter, heads, HD), -1)
    stats = jnp.concatenate(
        [glob_l[:, :HD], jnp.pad(glob_delta, ((0, 0), (0, HD - heads)))], 1
    )
    devices = data_count * seq_count
    piece = width // devices
    by_device = lambda grad: grad.reshape(devices, -1, width)

    def wide(grad):
        blocks = grad.reshape(devices, piece, -1, width)
        return blocks.transpose(0, 2, 1, 3).reshape(devices, -1, width)

    inner_rows = wide(grad_w_inner).shape[1]
    early_parts = jnp.concatenate([by_device(grad_w_outer), wide(grad_w_inner)], 1)
    planned = has_plan()
    sizes = BackSizes(
        block, count, quarter, seq_count, pairs, early_parts.shape[1] if planned else 0
    )
    query_low, key_low, value_low, dtab, *early = attend_back(
        sizes,
        lengths,
        table,
        queries,
        kx,
        vx,
        kg,
        vg,
        attn_low[:block],
        grad_attn[:block],
        long_l,
        glob_do,
        stats,
        *([by_core(early_parts)] if planned else []),
    )
    early = early[0] if planned else scattered(early_parts)
    own_normed, hat_one, inv_one = norm_forward(own_x, norm1_gain, norm1_shift)
    own_normed = own_normed.astype(BF16)
    grad_b_query = jnp.sum(query_low.astype(F32), 0)
    grad_b_value = jnp.sum(value_low.astype(F32), 0)
    grad_w_query = rows_dot(own_normed, query_low)
    grad_w_key = rows_dot(own_normed, key_low)
    grad_w_value = rows_dot(own_normed, value_low)
    grad_normed_one = (
        back_dot(query_low, w_query) + back_dot(key_low, w_key) + back_dot(value_low, w_value)
    )
    grad_from_one, grad_gain_one, grad_shift_one = norm_backward(
        grad_normed_one, hat_one, inv_one, norm1_gain
    )
    grad_x = grad_mid + grad_from_one

    g_outer = early[:-inner_rows]
    g_inner = early[-inner_rows:].reshape(-1, piece, width).transpose(1, 0, 2)
    vectors = (
        grad_b_query,
        grad_b_value,
        grad_b_out,
        grad_b_inner,
        grad_b_outer,
        grad_gain_one,
        grad_shift_one,
        grad_gain_two,
        grad_shift_two,
    )
    small = jnp.concatenate([v.reshape(devices, -1) for v in vectors], 1)
    small = jnp.pad(small, ((0, 0), (0, width - small.shape[1])))
    small = jnp.pad(small[:, None], ((0, 0), (0, 15), (0, 0)))
    late_parts = jnp.concatenate(
        [by_device(g) for g in (grad_w_query, grad_w_key, grad_w_value, grad_w_out)] + [small], 1
    )
    table_part = dtab.reshape(heads, WINDOW)
    if planned:
        late, table_total = reduce_late(by_core(late_parts), table_part)
    else:
        late, table_total = scattered(late_parts), lax.psum(table_part, ("dp", "seq"))
    table_total = table_total[:, HALO - R : HALO - R + labels].T
    pieces, at = [], 0
    for vector in vectors:
        length = vector.shape[0] // devices
        pieces.append(late[4 * piece, at : at + length])
        at += length
    g_b_query, g_b_value, g_b_out, g_b_inner, g_b_outer, g_g1, g_s1, g_g2, g_s2 = pieces
    g_query, g_key, g_value, g_out = (late[i * piece : (i + 1) * piece] for i in range(4))
    glob_out = lax.all_gather(result[block:].astype(BF16), "seq", axis=0, tiled=True)[:count]
    glob_grad = lax.all_gather(grad_x[block:], "seq", axis=0, tiled=True)[:count]
    return (
        long_result[None],
        glob_out[None],
        grad_x[:block][None],
        glob_grad[None],
        g_query,
        g_b_query,
        g_key,
        g_value,
        g_b_value,
        g_out,
        g_b_out,
        g_inner.reshape(piece, -1),
        g_b_inner,
        g_outer,
        g_b_outer,
        g_g1,
        g_s1,
        g_g2,
        g_s2,
        table_total,
    )


def solution(mesh):
    rows, whole = P("dp", "seq", None), P("dp", None, None)
    matrix, vector = P(("dp", "seq"), None), P(("dp", "seq"))
    return jax.shard_map(
        on_device,
        mesh=mesh,
        in_specs=(rows, whole, P("dp")) + (P(),) * 16 + (rows, whole),
        out_specs=(
            rows,
            whole,
            rows,
            whole,
            matrix,
            vector,
            matrix,
            matrix,
            vector,
            matrix,
            vector,
            matrix,
            vector,
            matrix,
            vector,
            vector,
            vector,
            vector,
            vector,
            P(),
        ),
        check_vma=False,
    )
```

profile of v0, /device:TPU:0, one launch (start us, length us, event | category | flops | bytes accessed | tf_op | source)
XLA Modules:
  0.0 276.1 jit_solution(11029065977462591524)
XLA Ops:
  11.6 29.8 %attend.1 = (bf16[768,768]{1,0:T(8,128)(2,1)}, bf16[768,768]{1,0:T(8,128)(2,1)}, bf16[768,768]{1,0:T(8,128)(2,1)}, bf16[256,768]{1,0:T(8,128)(2,1)}, bf16[256,76...) custom-call(s32[1]{0:T(128)} %copy.75.len_ref, ...), custom_call_target="tpu_custom_call" | custom-call | tf_op jit(solution)/shard_map/attend/pallas_call | solution.py:355
  41.3 2.2 slice.85.o_ref
  43.6 2.2 fusion.40
  46.5 3.0 %fusion.31 = f32[576,3072]{1,0:T(8,128)S(1)} fusion(bf16[768,3072]{1,0:T(8,128)(2,1)S(1)} %bitcast.105, f32[576,768]{1,0:T(8,128)S(1)} %get-tuple-element.140, f32[768]{0:T(1024)S(1)} %copy-done.29, f32[768]{0:T(1024)S(1)} %copy-done.23, f32[576]{0:T(1024)S(1)} %add_rsqrt_fusion.1, f32[576]{0:T(1024)S(1)} %broadcast_multiply_fusion.5), kind=kOutput, calls=%fused_computation.95 | convolution fusion | flops 2720120832 | bytes 13576704 | tf_op jit(solution)/shard_map/dot_general | solution.py:1007
  49.6 4.5 %add_add_fusion.1 = bf16[576,768]{1,0:T(8,128)(2,1)S(1)} fusion(f32[576,768]{1,0:T(8,128)S(1)} %get-tuple-element.140, bf16[3072,768]{1,0:T(8,128)(2,1)S(1)} %bitcast.103, f32[768]{0:T(1024)S(1)} %copy-done.28, f32[576,3072]{1,0:T(8,128)S(1)} %fusion.31, f32[3072]{0:T(1024)S(1)} %copy-done.26), kind=kOutput, calls=%fused_computation.39 | convolution fusion | flops 2736930816 | bytes 14466048 | tf_op jit(solution)/shard_map/dot_general | solution.py:1007
  54.1 6.9 %all_gather.6 = bf16[256,768]{1,0:T(8,128)(2,1)S(1)} all-gather(bf16[64,768]{1,0:T(8,128)(2,1)S(1)} %slice.138), channel_id=1, replica_groups=mesh['dp'=8,'seq'=4] {'seq'}, dimensions={0}, use_global_device_ids=true | all-gather | bytes 491520 | tf_op jit(solution)/shard_map/all_gather | solution.py:1193
  63.2 12.0 %fusion.41 = (bf16[3072]{0:T(1024)(128)(2,1)S(1)}, bf16[576,3072]{1,0:T(8,128)(2,1)}) fusion(f32[576,3072]{1,0:T(8,128)} %copy-done.30, f32[3072]{0:T(1024)S(1)} %copy-done.26, bf16[3072,768]{1,0:T(8,128)(2,1)} %param.33, bf16[64,768]{1,0:T(8,128)(2,1)S(1)} %get-tuple-element.119, bf16[512,768]{1,0:T(8,128)(2,1)S(1)} %get-tuple-element.121), kind=kOutput, calls=%fused_computation.102 | convolution fusion | flops 2758603776 | bytes 16238592 | tf_op jit(solution)/shard_map/dot_general | solution.py:1015
  75.2 10.4 %convolution_convert_fusion.1 = bf16[3072,768]{1,0:T(8,128)(2,1)} fusion(bf16[64,768]{1,0:T(8,128)(2,1)S(1)} %get-tuple-element.119, bf16[512,768]{1,0:T(8,128)(2,1)S(1)} %get-tuple-element.121, f32[576,3072]{1,0:T(8,128)} %copy-done.30, f32[3072]{0:T(1024)S(1)} %copy-done.26), kind=kOutput, calls=%fused_computation.13 | convolution fusion | flops 2739732480 | bytes 12693504 | tf_op jit(solution)/shard_map/rd,re->de/dot_general | solution.py:1011
  85.7 7.4 %multiply_reduce_fusion = (bf16[768]{0:T(1024)(128)(2,1)S(1)}, f32[576]{0:T(1024)S(1)}, f32[576]{0:T(1024)S(1)}, bf16[768]{0:T(1024)(128)(2,1)S(1)}, f32[576,768]{1,0:T(8,128)S(1)}) fusion(f32[576,768]{1,0:T(8,128)} %copy-done.3, f32[576]{0:T(1024)S(1)} %add_rsqrt_fusion.1, f32[576]{0:T(1024)S(1)} %broadcast_multiply_fusion.5, f32[768]{0:T(1024)S(1)} %copy-done.23, ...), kind=kOutput, calls=%fused_computation.32 | convolution fusion | flops 2721887744 | bytes 11811840 | tf_op jit(solution)/shard_map/dot_general | solution.py:1015
  93.1 2.0 fusion.37
  95.7 6.3 %convolution_convert_fusion = bf16[768,3072]{1,0:T(8,128)(2,1)} fusion(bf16[576,3072]{1,0:T(8,128)(2,1)S(1)} %copy-done.31, f32[576,768]{1,0:T(8,128)S(1)} %copy-done.4, f32[768]{0:T(1024)S(1)} %copy-done.29, f32[768]{0:T(1024)S(1)} %copy-done.23, f32[576]{0:T(1024)S(1)} %add_rsqrt_fusion.1, f32[576]{0:T(1024)S(1)} %broadcast_multiply_fusion.5), kind=kOutput, calls=%fused_computation.12 | convolution fusion | flops 2722480128 | bytes 10037760 | tf_op jit(solution)/shard_map/rd,re->de/dot_general | solution.py:1011
  102.0 9.8 %reshape.177 = bf16[32,24,4,768]{3,2,1,0:T(4,128)(2,1)} reshape(bf16[768,3072]{1,0:T(8,128)(2,1)} %convolution_convert_fusion) | data formatting | bytes 9437184 | tf_op jit(solution)/shard_map/reshape | solution.py:1120
  111.8 3.2 %copy.53 = bf16[32,24,4,768]{3,1,2,0:T(8,128)(2,1)S(1)} copy(bf16[32,24,4,768]{3,2,1,0:T(4,128)(2,1)} %reshape.177) | data formatting | bytes 9437184 | tf_op jit(solution)/shard_map/reshape | solution.py:1120
  115.0 6.6 %copy_bitcast_fusion.rest_0_ = bf16[2,4,2,2,192,768]{5,4,3,2,1,0:T(8,128)(2,1)} fusion(bf16[4,2,2,2,96,768]{5,4,3,2,1,0:T(8,128)(2,1)S(1)} %bitcast.79, bf16[4,2,2,2,96,768]{5,4,3,2,1,0:T(8,128)(2,1)} %bitcast.89), kind=kLoop, calls=%fused_computation.3 | loop fusion | flops 18874368 | bytes 18874368 | tf_op jit(solution)/shard_map/transpose | solution.py:659
  121.9 2.4 convolution_convert_fusion.6
  126.0 2.1 convolution_convert_fusion.2
  129.2 71.9 %attend_back.1 = (bf16[576,768]{1,0:T(8,128)(2,1)}, bf16[576,768]{1,0:T(8,128)(2,1)}, bf16[576,768]{1,0:T(8,128)(2,1)}, f32[6,2,512]{2,1,0:T(2,128)}, f32[192,768]{1,0:T(8,128)}) custom-call(s32[1]{0:T(128)} %copy.75.len_ref, f32[6,2,512]{2,1,0:T(2,128)} %reshape.175.tab_ref, bf16[768,768]{1,0:T(8,128)(2,1)} %get-tuple-element.36.q_ref, ...), custom_call_target="tpu_custom_call" | custom-call | tf_op jit(solution)/shard_map/attend_back/pallas_call | solution.py:992
  205.6 2.4 convolution_convert_fusion.4
  209.2 2.5 convolution_convert_fusion.5
  214.7 1.8 fusion.15
  216.9 2.7 convolution_convert_fusion.3
  220.9 8.9 %all_gather.7 = f32[256,768]{1,0:T(8,128)S(1)} all-gather(f32[64,768]{1,0:T(8,128)S(1)} %slice-done), channel_id=1, replica_groups=mesh['dp'=8,'seq'=4] {'seq'}, dimensions={0}, use_global_device_ids=true | all-gather | bytes 983040 | tf_op jit(solution)/shard_map/all_gather | solution.py:1194
  229.9 1.6 copy.63
  234.8 38.3 %reduce_late.1 = (f32[112,768]{1,0:T(8,128)S(1)}, f32[12,512]{1,0:T(8,128)S(1)}) custom-call(bf16[2,4,2,2,112,768]{5,4,3,2,1,0:T(8,128)(2,1)S(1)} %bitcast.78, f32[12,512]{1,0:T(8,128)S(1)} %reshape.187.table_ref), custom_call_target="tpu_custom_call" | custom-call | tf_op jit(solution)/shard_map/reduce_late/pallas_call | solution.py:632
  (139 shorter events, 32.7 us)
Async XLA Ops:
  0.7 42.9 %copy-start = (bf16[768,768]{1,0:T(8,128)(2,1)S(1)}, bf16[768,768]{1,0:T(8,128)(2,1)}, u32[]{:S(2)}) copy-start(bf16[768,768]{1,0:T(8,128)(2,1)} %param.29) | copy-start | bytes 3538948
  0.7 10.1 %copy-start.8 = (bf16[1,230,768]{2,1,0:T(8,128)(2,1)S(1)}, bf16[1,230,768]{2,1,0:T(8,128)(2,1)}, u32[]{:S(2)}) copy-start(bf16[1,230,768]{2,1,0:T(8,128)(2,1)} %param.22) | copy-start | bytes 1059844
  0.7 9.7 %copy-start.1 = (bf16[1,512,768]{2,1,0:T(8,128)(2,1)S(1)}, bf16[1,512,768]{2,1,0:T(8,128)(2,1)}, u32[]{:S(2)}) copy-start(bf16[1,512,768]{2,1,0:T(8,128)(2,1)} %param.21) | copy-start | bytes 2359300
  11.6 32.0 %copy-start.2 = (bf16[1,512,768]{2,1,0:T(8,128)(2,1)S(1)}, bf16[1,512,768]{2,1,0:T(8,128)(2,1)}, u32[]{:S(2)}) copy-start(bf16[1,512,768]{2,1,0:T(8,128)(2,1)} %param.21) | copy-start | bytes 2359300
  11.6 32.0 %copy-start.27 = (f32[768]{0:T(1024)S(1)}, f32[768]{0:T(1024)}, u32[]{:S(2)}) copy-start(f32[768]{0:T(1024)} %param.30) | copy-start | bytes 9220
  41.3 4.9 %slice-start.3 = ((s8[4718592]{0:T(1024)(128)(4,1)}), s8[4194304]{0:T(1024)(128)(4,1)S(1)}, s32[]{:S(2)}) async-start(s8[4718592]{0:T(1024)(128)(4,1)} %bitcast.104), calls=%async_computation.3 | async-start | bytes 8388608
  43.6 2.6 slice-start.4
  45.8 3.8 %copy-start.3 = (f32[576,768]{1,0:T(8,128)}, f32[576,768]{1,0:T(8,128)S(1)}, u32[]{:S(2)}) copy-start(f32[576,768]{1,0:T(8,128)S(1)} %get-tuple-element.140) | copy-start | bytes 5308420
  45.8 3.8 %slice-start.1 = ((s8[4718592]{0:T(1024)(128)(4,1)}), s8[4194304]{0:T(1024)(128)(4,1)S(1)}, s32[]{:S(2)}) async-start(s8[4718592]{0:T(1024)(128)(4,1)} %bitcast.102), calls=%async_computation.1 | async-start | bytes 8388608
  46.5 3.0 %slice-start.2 = ((s8[4718592]{0:T(1024)(128)(4,1)}), s8[524288]{0:T(1024)(128)(4,1)S(1)}, s32[]{:S(2)}) async-start(s8[4718592]{0:T(1024)(128)(4,1)} %bitcast.102), calls=%async_computation.2 | async-start | bytes 1048576
  46.5 3.1 %copy-start.26 = (f32[3072]{0:T(1024)S(1)}, f32[3072]{0:T(1024)}, u32[]{:S(2)}) copy-start(f32[3072]{0:T(1024)} %param.32) | copy-start | bytes 36868
  46.5 3.1 %copy-start.28 = (f32[768]{0:T(1024)S(1)}, f32[768]{0:T(1024)}, u32[]{:S(2)}) copy-start(f32[768]{0:T(1024)} %param.34) | copy-start | bytes 9220
  49.6 4.5 %copy-start.30 = (f32[576,3072]{1,0:T(8,128)}, f32[576,3072]{1,0:T(8,128)S(1)}, u32[]{:S(2)}) copy-start(f32[576,3072]{1,0:T(8,128)S(1)} %fusion.31) | copy-start | bytes 21233668
  54.1 7.7 %copy-start.18 = (bf16[1,512,768]{2,1,0:T(8,128)(2,1)S(1)}, bf16[1,512,768]{2,1,0:T(8,128)(2,1)}, u32[]{:S(2)}) copy-start(bf16[1,512,768]{2,1,0:T(8,128)(2,1)} %param.40) | copy-start | bytes 2359300
  85.7 7.4 %copy-start.4 = (f32[576,768]{1,0:T(8,128)S(1)}, f32[576,768]{1,0:T(8,128)}, u32[]{:S(2)}) copy-start(f32[576,768]{1,0:T(8,128)} %copy-done.3) | copy-start | bytes 5308420
  93.1 2.6 copy-start.31
  121.9 3.1 %copy-start.15 = (bf16[576,768]{1,0:T(8,128)(2,1)S(1)}, bf16[576,768]{1,0:T(8,128)(2,1)}, u32[]{:S(2)}) copy-start(bf16[576,768]{1,0:T(8,128)(2,1)} %get-tuple-element.35) | copy-start | bytes 2654212
  126.0 2.5 copy-start.20
  201.0 3.0 %copy-start.21 = (f32[6,2,512]{2,1,0:T(2,128)S(1)}, f32[6,2,512]{2,1,0:T(2,128)}, u32[]{:S(2)}) copy-start(f32[6,2,512]{2,1,0:T(2,128)} %get-tuple-element.46) | copy-start | bytes 73732
  201.1 3.0 %copy-start.19 = (f32[192,768]{1,0:T(8,128)S(1)}, f32[192,768]{1,0:T(8,128)}, u32[]{:S(2)}) copy-start(f32[192,768]{1,0:T(8,128)} %get-tuple-element.48) | copy-start | bytes 1769476
  201.1 4.5 %copy-start.22 = (f32[768]{0:T(1024)S(1)}, f32[768]{0:T(1024)}, u32[]{:S(2)}) copy-start(f32[768]{0:T(1024)} %param.35) | copy-start | bytes 9220
  201.1 4.5 %copy-start.24 = (f32[768]{0:T(1024)S(1)}, f32[768]{0:T(1024)}, u32[]{:S(2)}) copy-start(f32[768]{0:T(1024)} %param.36) | copy-start | bytes 9220
  209.2 2.5 copy-start.13
  216.9 2.7 copy-start.7
  (13 other events, 18.0 us)
where the time goes:
time: 281 us; the launch traced here: 276 us
  Pallas kernels  140 us (50%)
  matrix products  61.1 us (22%)
  local copies, waits for them, and re-layouts  38.2 us (14%)
  other arithmetic  18.5 us (7%)
  blocking collectives  15.8 us (6%)
    pallas_call x1, Pallas kernels, attend_back(): pl.pallas_call(functools.partial(back_kernel, sizes), grid=(2 * pairs,),...  71.9 us
    pallas_call x1, Pallas kernels, reduce_late(): pl.pallas_call(functools.partial(late_kernel, rows), in_specs=[pl.BlockSp...  38.3 us
    pallas_call x1, Pallas kernels, attend(): pl.pallas_call(functools.partial(attend_kernel, sizes), in_specs=[pl.Bloc...  29.8 us
    dot_general x6, matrix products, rows_dot(): return jnp.einsum('rd,re->de', left, right, preferred_element_type=F32)  26.4 us
    dot_general x6, matrix products, back_dot(): lax.dot_general(left, right, (((1,), (1,)), ((), ())), preferred_element_...  25 us
    reshape x2, local copies, waits for them, and re-layouts, wide(): blocks = grad.reshape(devices, piece, -1, width)  13 us
    dot_general x3, matrix products, matmul(): return jnp.dot(left, right, preferred_element_type=F32)  9.67 us
    all_gather x1, blocking collectives, on_device(): lax.all_gather(grad_x[block:], 'seq', axis=0, tiled=True)[:count]  8.92 us

commit v1 on v0

--- a/solution.py
+++ b/solution.py
@@ -384,22 +384,16 @@
 
 
 class Reducer:
-    def __init__(self, mesh_ids, rows, pieces, mine, from_core, from_one, from_two, from_z, sems):
-        self.ids = mesh_ids
+    def __init__(self, rows, scratch, pieces=None, outgoing=None):
+        self.ids = mesh_ids()
         half = (rows // 2 + 15) // 16 * 16
         self.halves = (slice(0, half), slice(half, rows))
-        self.pieces, self.mine = pieces, mine
-        self.from_core, self.from_one, self.from_two, self.from_z = (
-            from_core,
-            from_one,
-            from_two,
-            from_z,
-        )
-        self.local, self.sends, self.recvs = sems
+        self.pieces, self.outgoing = pieces, outgoing
+        self.mine, self.from_core, self.from_one, self.from_two, self.from_z = scratch[:5]
+        self.local, self.sends, self.recvs = scratch[5:]
 
     @staticmethod
     def scratch(rows, width):
-        half = (rows // 2 + 15) // 16 * 16
         return [
             pltpu.VMEM((4, 2, 2, rows, width), BF16),
             pltpu.VMEM((4, 2, 2, rows, width), BF16),
@@ -418,40 +412,50 @@
         return near + [(lax.rem(z + step, 4) * 2 + y, seq) for step in (1, 2, 3)]
 
     def target(self, chunk):
-        return lax.rem(self.ids[0] + 1 + chunk, 4)
-
-    def remote(self, source, dest, kind, chunk, partner):
+        return chunk if self.pieces is None else lax.rem(self.ids[0] + 1 + chunk, 4)
+
+    def remote(self, source, dest, kind, send_at, recv_at, device):
         return pltpu.make_async_remote_copy(
             src_ref=source,
             dst_ref=dest,
-            send_sem=self.sends.at[kind, chunk],
-            recv_sem=self.recvs.at[kind, chunk],
-            device_id=self.partners()[partner],
+            send_sem=self.sends.at[kind, send_at],
+            recv_sem=self.recvs.at[kind, recv_at],
+            device_id=device,
             device_id_type=pl.DeviceIdType.MESH,
         )
 
     def own_copy(self, chunk):
-        z, y, x, core = self.ids
-        to = self.target(chunk)
+        core, to = self.ids[3], self.target(chunk)
         return pltpu.make_async_copy(
             self.pieces.at[core, to], self.mine.at[to], self.local.at[chunk]
         )
 
     def core_copy(self, chunk):
-        z, y, x, core = self.ids
-        to = self.target(chunk)
-        return self.remote(self.pieces.at[1 - core, to], self.from_core.at[to], 0, chunk, 0)
+        core, to = self.ids[3], self.target(chunk)
+        source = self.outgoing.at[to] if self.pieces is None else self.pieces.at[1 - core, to]
+        return self.remote(source, self.from_core.at[to], 0, chunk, chunk, self.partners()[0])
 
     def first_copies(self, chunk):
         z, y, x, core = self.ids
         to = self.target(chunk)
         one, two = self.halves
+        near = self.partners()
         return (
             self.remote(
-                self.mine.at[to, :, 1 - x, one], self.from_one.at[to, :, one], 1, chunk, 1
+                self.mine.at[to, :, 1 - x, one],
+                self.from_one.at[to, :, one],
+                1,
+                chunk,
+                chunk,
+                near[1],
             ),
             self.remote(
-                self.mine.at[to, 1 - y, :, two], self.from_one.at[to, :, two], 2, chunk, 2
+                self.mine.at[to, 1 - y, :, two],
+                self.from_one.at[to, :, two],
+                2,
+                chunk,
+                chunk,
+                near[2],
             ),
         )
 
@@ -459,29 +463,57 @@
         z, y, x, core = self.ids
         to = self.target(chunk)
         one, two = self.halves
+        near = self.partners()
         return (
             self.remote(
-                self.mine.at[to, 1 - y, x, one], self.from_two.at[to, one], 3, chunk, 2
+                self.mine.at[to, 1 - y, x, one],
+                self.from_two.at[to, one],
+                3,
+                chunk,
+                chunk,
+                near[2],
             ),
             self.remote(
-                self.mine.at[to, y, 1 - x, two], self.from_two.at[to, two], 4, chunk, 1
+                self.mine.at[to, y, 1 - x, two],
+                self.from_two.at[to, two],
+                4,
+                chunk,
+                chunk,
+                near[1],
             ),
         )
 
     def last_copy(self, chunk):
         z, y, x, core = self.ids
+        to = self.target(chunk)
+        slot = lax.rem(z - to + 4, 4) - 1
         return self.remote(
-            self.mine.at[self.target(chunk), y, x], self.from_z.at[chunk], 5, chunk, 3 + chunk
+            self.mine.at[to, y, x],
+            self.from_z.at[slot],
+            5,
+            chunk,
+            slot,
+            (to * 2 + y, x * 2 + core),
         )
 
-    def start(self):
-        for chunk in range(4):
-            self.core_copy(chunk).start()
+    def arrival(self, slot):
+        z, y, x, core = self.ids
+        return self.remote(
+            self.mine.at[z, y, x], self.from_z.at[slot], 5, slot, slot, self.partners()[3]
+        )
+
+    def leaves(self, chunk):
+        return chunk < 3 if self.pieces is not None else self.target(chunk) != self.ids[0]
+
+    def start(self, chunk):
+        self.core_copy(chunk).start()
+        if self.pieces is not None:
             self.own_copy(chunk).start()
 
     def add_core(self, chunk):
         to = self.target(chunk)
-        self.own_copy(chunk).wait()
+        if self.pieces is not None:
+            self.own_copy(chunk).wait()
         self.core_copy(chunk).wait_recv()
 
         def add(index, carry):
@@ -519,7 +551,9 @@
         to = self.target(chunk)
         for copy in self.second_copies(chunk):
             copy.wait_recv()
-        if chunk < 3:
+
+        @pl.when(self.leaves(chunk))
+        def _():
             self.mine[to, y, x] = (
                 self.mine[to, y, x].astype(F32) + self.from_two[to].astype(F32)
             ).astype(BF16)
@@ -528,15 +562,17 @@
     def finish(self, out):
         z, y, x, core = self.ids
         total = self.mine[z, y, x].astype(F32) + self.from_two[z].astype(F32)
-        for chunk in range(3):
-            self.last_copy(chunk).wait_recv()
-            total += self.from_z[chunk].astype(F32)
+        for slot in range(3):
+            self.arrival(slot).wait_recv()
+            total += self.from_z[slot].astype(F32)
         out[...] = total
         for chunk in range(4):
             self.core_copy(chunk).wait_send()
             for copy in self.first_copies(chunk) + self.second_copies(chunk):
                 copy.wait_send()
-            if chunk < 3:
+
+            @pl.when(self.leaves(chunk))
+            def _(chunk=chunk):
                 self.last_copy(chunk).wait_send()
 
 
@@ -553,18 +589,18 @@
 
 
 EARLY_PLAN = (
-    (1, "add_core", 0),
-    (2, "add_core", 1),
-    (3, "add_core", 2),
-    (4, "add_core", 3),
-    (5, "add_first", 0),
+    (2, "add_core", 0),
+    (3, "add_core", 1),
+    (4, "add_core", 2),
+    (5, "add_core", 3),
+    (7, "add_first", 0),
     (8, "add_first", 1),
     (9, "add_second", 0),
-    (11, "add_first", 2),
-    (11, "add_second", 1),
+    (10, "add_first", 2),
+    (10, "add_second", 1),
     (11, "add_first", 3),
-    (11, "add_second", 2),
-    (11, "add_second", 3),
+    (12, "add_second", 2),
+    (12, "add_second", 3),
 )
 LATE_PLAN = (
     ("add_core", 0),
@@ -583,7 +619,7 @@
 
 
 def late_kernel(rows, pieces_ref, table_ref, out_ref, total_ref, *scratch):
-    reducer = Reducer(mesh_ids(), rows, pieces_ref, *scratch[:5], scratch[5:8])
+    reducer = Reducer(rows, scratch[:8], pieces=pieces_ref)
     kept, arrived, sends, recvs = scratch[8:]
     z, y, x, core = mesh_ids()
     dp, seq = lax.axis_index("dp"), lax.axis_index("seq")
@@ -608,7 +644,8 @@
         )
 
     meet(reducer.partners())
-    reducer.start()
+    for chunk in range(4):
+        reducer.start(chunk)
     kept[0] = table_ref[...]
     table_copy(0).start()
     for number, (act, chunk) in enumerate(LATE_PLAN):
@@ -659,23 +696,334 @@
     return parts.astype(BF16).reshape((4, 2, 2, 2) + parts.shape[1:]).transpose(3, 0, 1, 2, 4, 5)
 
 
-def scattered(parts):
-    return lax.psum_scatter(
-        parts.astype(BF16), ("dp", "seq"), scatter_dimension=0, tiled=True
-    )[0].astype(F32)
-
-
-class BackSizes(NamedTuple):
-    block: int
-    count: int
-    quarter: int
-    seq_count: int
-    pairs: int
-    early_rows: int
+GELU_A = 0.7978845608028654
+GELU_B = 0.044715
+
+
+def gate_both(u):
+    square = u * u
+    turned = jnp.tanh(GELU_A * u * (1.0 + GELU_B * square))
+    half = 0.5 * (1.0 + turned)
+    slope = half + 0.5 * u * (1.0 - turned * turned) * (
+        GELU_A * (1.0 + 3.0 * GELU_B * square)
+    )
+    return u * half, slope
+
+
+def column_sum(rows):
+    return jnp.sum(rows, 0, keepdims=True)
+
+
+def ffn_kernel(
+    sizes,
+    planned,
+    len_ref,
+    attn_ref,
+    long_ref,
+    glob_ref,
+    dlong_ref,
+    dglob_ref,
+    lq_ref,
+    wo_ref,
+    bo_ref,
+    gain_ref,
+    shift_ref,
+    wi_ref,
+    bi_ref,
+    wr_ref,
+    br_ref,
+    long_out,
+    glob_out,
+    dmid_ref,
+    do_ref,
+    dog_ref,
+    ldg_ref,
+    *rest,
+):
+    block, count, quarter, seq_count, pairs = sizes
+    if planned:
+        pieces_ref, sum_ref, *rest = rest
+    else:
+        g_outer_ref, g_inner_ref, g_out_ref, vec_ref, *rest = rest
+    (
+        mid,
+        y_sum,
+        df_sum,
+        normed,
+        normed_t,
+        dy,
+        vectors,
+        every_do,
+        every_ld,
+        every_out,
+        gather_sends,
+        gather_recvs,
+        *rest,
+    ) = rest
+    if planned:
+        even, odd, outgoing, *rest = rest
+        reducer = Reducer(outgoing.shape[-2], rest, outgoing=outgoing)
+    chunk = pl.program_id(0)
+    seq_index = lax.axis_index("seq")
+    own_rows = pl.ds(pl.multiple_of(seq_index * quarter, quarter), quarter)
+    width = mid.shape[1]
+
+    def gathers():
+        for step in range(1, seq_count):
+            for kind, every in enumerate((every_do, every_ld, every_out)):
+                yield kind, pltpu.make_async_remote_copy(
+                    src_ref=every.at[own_rows],
+                    dst_ref=every.at[own_rows],
+                    send_sem=gather_sends.at[kind, step - 1],
+                    recv_sem=gather_recvs.at[kind, step - 1],
+                    device_id=seq_device(step, seq_count),
+                    device_id_type=pl.DeviceIdType.MESH,
+                )
+
+    @pl.when(chunk == 0)
+    def _():
+        others = [seq_device(step, seq_count) for step in range(1, seq_count)]
+        meet(others + (reducer.partners()[2:] if planned else []))
+        projected = dot_n(attn_ref[...], wo_ref[...]) + bo_ref[...]
+        mid[:block] = long_ref[...].astype(F32) + projected[:block]
+        mid[block:] = glob_ref[own_rows].astype(F32) + projected[block:]
+        hat, _ = row_norm(mid[...])
+        normed[...] = (hat * gain_ref[...] + shift_ref[...]).astype(BF16)
+        normed_t[...] = normed[...].T
+        y_sum[...] = mid[...] + br_ref[...]
+        df_sum[...] = jnp.zeros_like(df_sum)
+        position = seq_index * block + lax.broadcasted_iota(jnp.int32, (block, 1), 0)
+        dy[:block] = jnp.where(
+            position < len_ref[0], dlong_ref[...].astype(F32), 0.0
+        ).astype(BF16)
+        dy[block:] = dglob_ref[own_rows]
+        vectors[1:2] = column_sum(dy[...].astype(F32))
+
+    if planned:
+        for now, act, at in OUTER_PLAN:
+
+            @pl.when(chunk == now)
+            def _(act=act, at=at):
+                getattr(reducer, act)(at)
+
+    active, slope = gate_both(dot_n(normed[...], wi_ref[...]) + bi_ref[...])
+    active = active.astype(BF16)
+    g_outer = t_dot(active, dy[...])
+    if planned:
+        core = reducer.ids[3]
+        rows = g_outer.shape[0] // 8
+        for part in range(4):
+            for side in range(2):
+                at = (2 * part + side) * rows
+                value = g_outer[at : at + rows].astype(BF16)
+
+                @pl.when(core == side)
+                def _(part=part, value=value):
+                    reducer.mine[chunk, part // 2, part % 2] = value
+
+                @pl.when(core != side)
+                def _(part=part, value=value):
+                    outgoing[chunk, part // 2, part % 2] = value
+
+        reducer.start(chunk)
+    else:
+        g_outer_ref[...] = g_outer.astype(BF16)
+    y_sum[...] += dot_n(active, wr_ref[...])
+    hidden = dot_t(dy[...], wr_ref[...]) * slope
+    for at in range(4):
+
+        @pl.when(chunk == at)
+        def _(at=at):
+            vectors[4 + at : 5 + at] = column_sum(hidden)
+
+    hidden = hidden.astype(BF16)
+    df_sum[...] += dot_t(hidden, wi_ref[...])
+    g_inner = dot_n(normed_t[...], hidden)
+    if planned:
+        piece = width // 32
+        for now in range(4):
+
+            @pl.when(chunk == now)
+            def _(now=now):
+                (even, odd)[now % 2][...] = g_inner
+                if now % 2 == 1:
+
+                    def pack(at, carry):
+                        rows = pl.ds(pl.multiple_of(at * piece, 8), piece)
+                        where = (
+                            lax.rem(at, 2),
+                            lax.div(at, 8),
+                            lax.rem(lax.div(at, 4), 2),
+                            lax.rem(lax.div(at, 2), 2),
+                        )
+                        pieces_ref[where + (slice(now // 2 * 48, now // 2 * 48 + 48),)] = (
+                            jnp.concatenate([even[rows], odd[rows]], 0).astype(BF16)
+                        )
+                        return carry
+
+                    lax.fori_loop(0, 32, pack, 0)
+    else:
+        g_inner_ref[...] = g_inner.astype(BF16)
+
+    @pl.when(chunk == 3)
+    def _():
+        position = seq_index * block + lax.broadcasted_iota(jnp.int32, (block, 1), 0)
+        long_out[...] = jnp.where(position < len_ref[0], y_sum[:block], 0.0).astype(BF16)
+        every_out[own_rows] = y_sum[block:].astype(BF16)
+        hat, inverse = row_norm(mid[...])
+        df = df_sum[...]
+        vectors[2:3] = column_sum(df * hat)
+        vectors[3:4] = column_sum(df)
+        scaled = df * gain_ref[...]
+        dmid = dy[...].astype(F32) + inverse * (
+            scaled
+            - jnp.mean(scaled, -1, keepdims=True)
+            - hat * jnp.mean(scaled * hat, -1, keepdims=True)
+        )
+        dmid_ref[...] = dmid
+        vectors[0:1] = column_sum(dmid)
+        low = dmid.astype(BF16)
+        grad_o = dot_t(low, wo_ref[...]).astype(BF16)
+        do_ref[...] = grad_o
+        every_do[own_rows] = grad_o[block:]
+        both = grad_o[block:].astype(F32) * attn_ref[block:].astype(F32)
+        stats = lq_ref[...]
+        for head in range(2 * pairs):
+            lanes = slice(head // 2 * PAIR, head // 2 * PAIR + PAIR)
+            delta = jnp.sum(own_half(head % 2, both[:, lanes]), -1, keepdims=True)
+            stats = jnp.where(lane_index() == HD + head, delta, stats)
+        every_ld[own_rows] = stats
+        for _, copy in gathers():
+            copy.start()
+        g_out = t_dot(attn_ref[...], low)
+        if planned:
+            even[...] = g_out
+            piece = width // 32
+
+            def pack(at, carry):
+                rows = pl.ds(pl.multiple_of(at * piece, 8), piece)
+                where = (
+                    lax.rem(at, 2),
+                    lax.div(at, 8),
+                    lax.rem(lax.div(at, 4), 2),
+                    lax.rem(lax.div(at, 2), 2),
+                )
+                pieces_ref[where + (slice(96, 128),)] = jnp.concatenate(
+                    [even[rows], vectors[...]], 0
+                ).astype(BF16)
+                return carry
+
+            lax.fori_loop(0, 32, pack, 0)
+            for now, act, at in OUTER_PLAN:
+                if now == 4:
+                    getattr(reducer, act)(at)
+            reducer.finish(sum_ref)
+        else:
+            g_out_ref[...] = g_out.astype(BF16)
+            vec_ref[...] = vectors[...]
+        for _, copy in gathers():
+            copy.wait_recv()
+        dog_ref[...] = every_do[...]
+        ldg_ref[...] = every_ld[...]
+        glob_out[...] = every_out[...]
+        for _, copy in gathers():
+            copy.wait_send()
+
+
+OUTER_PLAN = (
+    (1, "add_core", 0),
+    (2, "add_first", 0),
+    (2, "add_core", 1),
+    (3, "add_second", 0),
+    (3, "add_first", 1),
+    (3, "add_core", 2),
+    (4, "add_core", 3),
+    (4, "add_second", 1),
+    (4, "add_first", 2),
+    (4, "add_second", 2),
+    (4, "add_first", 3),
+    (4, "add_second", 3),
+)
+
+
+def feed_forward(sizes, planned, doc_len, attn, long_x, glob_x, dlong, dglob, lq, *weights):
+    block, count, quarter, seq_count, pairs = sizes
+    wo, bo, gain, shift, wi, bi, wr, br = weights
+    width, hidden = wi.shape
+    chunk = hidden // 4
+    rows = block + quarter
+    whole = pl.BlockSpec(memory_space=pltpu.VMEM)
+    shape = jax.ShapeDtypeStruct
+    in_specs = [pl.BlockSpec(memory_space=pltpu.SMEM)] + [whole] * 10
+    in_specs += [
+        pl.BlockSpec((width, chunk), lambda c: (0, c)),
+        pl.BlockSpec((1, chunk), lambda c: (0, c)),
+        pl.BlockSpec((chunk, width), lambda c: (c, 0)),
+        whole,
+    ]
+    outs = [
+        shape((block, width), BF16),
+        shape((GP, width), BF16),
+        shape((rows, width), F32),
+        shape((rows, width), BF16),
+        shape((GP, width), BF16),
+        shape((GP, PAIR), F32),
+    ]
+    out_specs = [whole] * 6
+    others = seq_count - 1
+    scratch = [
+        pltpu.VMEM((rows, width), F32),
+        pltpu.VMEM((rows, width), F32),
+        pltpu.VMEM((rows, width), F32),
+        pltpu.VMEM((rows, width), BF16),
+        pltpu.VMEM((width, rows), BF16),
+        pltpu.VMEM((rows, width), BF16),
+        pltpu.VMEM((8, width), F32),
+        pltpu.VMEM((GP, width), BF16),
+        pltpu.VMEM((GP, PAIR), F32),
+        pltpu.VMEM((GP, width), BF16),
+        pltpu.SemaphoreType.DMA((3, others)),
+        pltpu.SemaphoreType.DMA((3, others)),
+    ]
+    if planned:
+        part = hidden // 32
+        outs += [shape((2, 4, 2, 2, part + width // 32 + 8, width), BF16), shape((part, width), F32)]
+        out_specs += [whole] * 2
+        scratch += [
+            pltpu.VMEM((width, chunk), F32),
+            pltpu.VMEM((width, chunk), F32),
+            pltpu.VMEM((4, 2, 2, part, width), BF16),
+        ] + Reducer.scratch(part, width)
+    else:
+        outs += [
+            shape((hidden, width), BF16),
+            shape((width, hidden), BF16),
+            shape((width, width), BF16),
+            shape((8, width), F32),
+        ]
+        out_specs += [
+            pl.BlockSpec((chunk, width), lambda c: (c, 0)),
+            pl.BlockSpec((width, chunk), lambda c: (0, c)),
+            whole,
+            whole,
+        ]
+    return pl.pallas_call(
+        functools.partial(ffn_kernel, sizes, planned),
+        grid=(4,),
+        in_specs=in_specs,
+        out_specs=out_specs,
+        out_shape=outs,
+        scratch_shapes=scratch,
+        compiler_params=pltpu.CompilerParams(
+            collective_id=4, has_side_effects=True, vmem_limit_bytes=62 * 2**20
+        ),
+        name="feed_forward",
+    )(doc_len, attn, long_x, glob_x, dlong, dglob, lq, wo, bo, gain, shift, wi, bi, wr, br)
 
 
 def back_kernel(
     sizes,
+    early_rows,
     len_ref,
     tab_ref,
     q_ref,
@@ -686,11 +1034,11 @@
     o_ref,
     do_ref,
     l_ref,
-    doq_ref,
-    ldq_ref,
+    dog_ref,
+    ldg_ref,
     *rest,
 ):
-    block, count, quarter, seq_count, pairs, early_rows = sizes
+    block, count, quarter, seq_count, pairs = sizes
     reduces = early_rows > 0
     if reduces:
         pieces_ref, rest = rest[0], rest[1:]
@@ -702,14 +1050,12 @@
         dvx,
         dkg,
         dvg,
-        glob_send,
-        glob_recv,
+        q_send,
+        q_recv,
+        kv_send,
+        kv_recv,
         halo_send,
         halo_recv,
-        dog_all,
-        ld_all,
-        every_sends,
-        every_recvs,
         glob_sends,
         glob_recvs,
         halo_sends,
@@ -719,42 +1065,31 @@
     number = pl.program_id(0)
     pair = lax.rem(number, pairs)
     seq_index = lax.axis_index("seq")
-    reducer = Reducer(mesh_ids(), early_rows, pieces_ref, *rest[:5], rest[5:]) if reduces else None
+    reducer = Reducer(early_rows, rest, pieces=pieces_ref) if reduces else None
     scale = HD ** (-0.5)
     low_lanes = lane_index() < HD
     own_keys = slice(HALO, HALO + block)
     own_rows = pl.ds(pl.multiple_of(seq_index * quarter, quarter), quarter)
 
-    def every_copies():
-        for step in range(1, seq_count):
-            for kind, (source, dest) in enumerate(((doq_ref, dog_all), (ldq_ref, ld_all))):
-                yield pltpu.make_async_remote_copy(
-                    src_ref=source,
-                    dst_ref=dest.at[seq_index],
-                    send_sem=every_sends.at[kind, step - 1],
-                    recv_sem=every_recvs.at[kind, step - 1],
-                    device_id=seq_device(step, seq_count),
-                    device_id_type=pl.DeviceIdType.MESH,
-                )
-
-    def glob_copies(at):
+    def glob_copies(kind, at):
+        source, dest = ((q_send, q_recv), (kv_send, kv_recv))[kind]
         for step in range(1, seq_count):
             device = seq_device(step, seq_count)
             yield pltpu.make_async_remote_copy(
-                src_ref=glob_send.at[device[1], at],
-                dst_ref=glob_recv.at[step - 1, at],
-                send_sem=glob_sends.at[step - 1, at],
-                recv_sem=glob_recvs.at[step - 1, at],
+                src_ref=source.at[device[1], at],
+                dst_ref=dest.at[step - 1, at],
+                send_sem=glob_sends.at[kind, step - 1, at],
+                recv_sem=glob_recvs.at[kind, step - 1, at],
                 device_id=device,
                 device_id_type=pl.DeviceIdType.MESH,
             )
 
-    def halo_copy(direction):
+    def halo_copy(direction, at):
         return pltpu.make_async_remote_copy(
-            src_ref=halo_send.at[direction],
-            dst_ref=halo_recv.at[direction],
-            send_sem=halo_sends.at[direction],
-            recv_sem=halo_recvs.at[direction],
+            src_ref=halo_send.at[direction, at],
+            dst_ref=halo_recv.at[direction, at],
+            send_sem=halo_sends.at[direction, at],
+            recv_sem=halo_recvs.at[direction, at],
             device_id=seq_device(2 * direction - 1, seq_count),
             device_id_type=pl.DeviceIdType.MESH,
         )
@@ -762,26 +1097,108 @@
     has_low, has_high = seq_index > 0, seq_index < seq_count - 1
     sends_to = (has_low, has_high)
     gets_from = (has_high, has_low)
+
+    def close_pair(at):
+        lanes = lanes_of(at)
+        for direction in range(2):
+
+            @pl.when(gets_from[direction])
+            def _(direction=direction):
+                halo_copy(direction, at).wait_recv()
+
+        for kind, (total, out) in enumerate(((dkx, dk_ref), (dvx, dv_ref))):
+            first, last = HALO + REACH, HALO + block - REACH
+            out[:REACH, lanes] = (
+                total[at, HALO:first] + halo_recv[1, at, kind].astype(F32)
+            ).astype(BF16)
+            out[REACH : block - REACH, lanes] = total[at, first:last].astype(BF16)
+            out[block - REACH : block, lanes] = (
+                total[at, last : HALO + block] + halo_recv[0, at, kind].astype(F32)
+            ).astype(BF16)
+        sums = []
+        for kind, (source, dest) in enumerate(((q_send, q_recv), (kv_send, kv_recv))):
+            total = source[seq_index, at].astype(F32)
+            for step, copy in enumerate(glob_copies(kind, at)):
+                copy.wait_recv()
+                total += dest[step, at].astype(F32)
+            sums.append(total.astype(BF16))
+        dq_ref[block:, lanes] = sums[0]
+        dk_ref[block:, lanes] = sums[1][:, :PAIR]
+        dv_ref[block:, lanes] = sums[1][:, PAIR:]
+
+    def run_plan(now):
+        for at, act, chunk in EARLY_PLAN:
+            if now == at:
+                getattr(reducer, act)(chunk)
 
     @pl.when(number == 0)
     def _():
         others = [seq_device(step, seq_count) for step in range(1, seq_count)]
         meet(others + (reducer.partners()[2:] if reduces else []))
-        for copy in every_copies():
+        if reduces:
+            for chunk in range(4):
+                reducer.start(chunk)
+        for direction in range(2):
+
+            @pl.when(jnp.logical_not(gets_from[direction]))
+            def _(direction=direction):
+                halo_recv[direction] = jnp.zeros_like(halo_recv[direction])
+
+    if reduces:
+        for now in range(1, 2 * pairs):
+            if any(at == now for at, _, _ in EARLY_PLAN):
+
+                @pl.when(number == now)
+                def _(now=now):
+                    run_plan(now)
+
+    @pl.when(number < pairs)
+    def _():
+        long_bias = key_bias(seq_index * block, block, len_ref[0])
+        near_bias = key_bias(seq_index * quarter, quarter, count)
+        query = q_ref[block:] * jnp.asarray(scale, BF16)
+        grad_o = dog_ref[...]
+        far_k, far_v = kx_ref[own_keys], vx_ref[own_keys]
+        near_k, near_v = kg_ref[own_rows], vg_ref[own_rows]
+        outs, kept = [], []
+        for head in range(2):
+            norm = in_three(-pick_column(ldg_ref[...], 2 * pair + head))
+            delta = in_three(-pick_column(ldg_ref[...], HD + 2 * pair + head))
+            qa = with_lanes(head, query, (1.0,) + norm)
+            doa = with_lanes(head, grad_o, delta)
+            far = jnp.exp(dot_t(qa, key_side(head, far_k, long_bias)))
+            near = jnp.exp(dot_t(qa, key_side(head, near_k, near_bias)))
+            far_ds = (far * dot_t(doa, value_side(head, far_v))).astype(BF16)
+            near_ds = (near * dot_t(doa, value_side(head, near_v))).astype(BF16)
+            outs.append(dot_n(far_ds, far_k) + dot_n(near_ds, near_k))
+            kept.append(
+                (
+                    own_half(head, query),
+                    own_half(head, grad_o),
+                    far.astype(BF16),
+                    near.astype(BF16),
+                    far_ds,
+                    near_ds,
+                )
+            )
+        own_q, own_do, far, near, far_ds, near_ds = (
+            jnp.concatenate(part, 0) for part in zip(*kept)
+        )
+        for total, edge in ((dkx, own_keys), (dvx, own_keys)):
+            total[pair, :HALO] = jnp.zeros((HALO, PAIR), F32)
+            total[pair, HALO + block :] = jnp.zeros((HALO, PAIR), F32)
+        dkx[pair, own_keys] = t_dot(far_ds, own_q)
+        dvx[pair, own_keys] = t_dot(far, own_do)
+        dkg[pair] = jnp.zeros((GP, PAIR), F32)
+        dvg[pair] = jnp.zeros((GP, PAIR), F32)
+        dkg[pair, own_rows] = t_dot(near_ds, own_q)
+        dvg[pair, own_rows] = t_dot(near, own_do)
+        glob_dq = (jnp.where(low_lanes, outs[0], outs[1]) * scale).astype(BF16)
+        q_send[:, pair] = glob_dq.reshape(seq_count, quarter, PAIR)
+        for copy in glob_copies(0, pair):
             copy.start()
-        if reduces:
-            reducer.start()
-        dog_all[seq_index] = doq_ref[...]
-        ld_all[seq_index] = ldq_ref[...]
-
-    if reduces:
-        for at, act, chunk in EARLY_PLAN:
-
-            @pl.when(number == at)
-            def _(act=act, chunk=chunk):
-                getattr(reducer, act)(chunk)
-
-    @pl.when(number < pairs)
+
+    @pl.when(number >= pairs)
     def _():
         long_bias = key_bias(seq_index * block - HALO, block + 2 * HALO, len_ref[0])
         glob_bias = key_bias(0, GP, count)
@@ -805,8 +1222,6 @@
                     bias=band_bias(tab_ref[0, head : head + 1]),
                 )
             )
-        dkx[pair] = jnp.zeros_like(dkx[pair])
-        dvx[pair] = jnp.zeros_like(dvx[pair])
         table_sums = [0.0, 0.0]
         grads_q = []
         for start in range(0, block, SUB):
@@ -829,121 +1244,54 @@
             band_ds, glob_ds = (jnp.concatenate(part, 0) for part in zip(*grads))
             dkx[pair, keys] += t_dot(band_ds, own_q)
             dvx[pair, keys] += t_dot(band, own_do)
-            more_k, more_v = t_dot(glob_ds, own_q), t_dot(glob, own_do)
-            dkg[pair] = more_k if start == 0 else dkg[pair] + more_k
-            dvg[pair] = more_v if start == 0 else dvg[pair] + more_v
+            dkg[pair] += t_dot(glob_ds, own_q)
+            dvg[pair] += t_dot(glob, own_do)
+        for kind, total in enumerate((dkg, dvg)):
+            kv_send[:, pair, :, kind * PAIR : (kind + 1) * PAIR] = (
+                total[pair].astype(BF16).reshape(seq_count, quarter, PAIR)
+            )
+        for copy in glob_copies(1, pair):
+            copy.start()
+        for kind, total in enumerate((dkx, dvx)):
+            for direction, first in enumerate((HALO - REACH, HALO + block)):
+                halo_send[direction, pair, kind] = total[pair, first : first + REACH].astype(BF16)
+        for direction in range(2):
+
+            @pl.when(sends_to[direction])
+            def _(direction=direction):
+                halo_copy(direction, pair).start()
+
         dq_ref[:block, lanes_of(pair)] = (jnp.concatenate(grads_q, 0) * scale).astype(BF16)
         for head in range(2):
             dtab_ref[pair, head : head + 1] = diagonal_sums(table_sums[head])
 
-    @pl.when(number == pairs)
+    @pl.when(number > pairs)
     def _():
-        for kind, total in enumerate((dkx, dvx)):
-            for direction, first in enumerate((HALO - REACH, HALO + block)):
-                halo_send[direction, kind] = total[:, first : first + REACH].astype(BF16)
-        for direction in range(2):
-
-            @pl.when(sends_to[direction])
-            def _(direction=direction):
-                halo_copy(direction).start()
-
-        for copy in every_copies():
-            copy.wait_recv()
-
-    @pl.when(number >= pairs)
-    def _():
-        long_bias = key_bias(seq_index * block, block, len_ref[0])
-        near_bias = key_bias(seq_index * quarter, quarter, count)
-        query = q_ref[block:] * jnp.asarray(scale, BF16)
-        grad_o = dog_all[:, :, lanes_of(pair)].reshape(GP, PAIR)
-        stats = ld_all[...].reshape(GP, PAIR)
-        far_k, far_v = kx_ref[own_keys], vx_ref[own_keys]
-        near_k, near_v = kg_ref[own_rows], vg_ref[own_rows]
-        outs, kept = [], []
-        for head in range(2):
-            norm = in_three(-pick_column(stats, 2 * pair + head))
-            delta = in_three(-pick_column(stats, HD + 2 * pair + head))
-            qa = with_lanes(head, query, (1.0,) + norm)
-            doa = with_lanes(head, grad_o, delta)
-            far = jnp.exp(dot_t(qa, key_side(head, far_k, long_bias)))
-            near = jnp.exp(dot_t(qa, key_side(head, near_k, near_bias)))
-            far_ds = (far * dot_t(doa, value_side(head, far_v))).astype(BF16)
-            near_ds = (near * dot_t(doa, value_side(head, near_v))).astype(BF16)
-            outs.append(dot_n(far_ds, far_k) + dot_n(near_ds, near_k))
-            kept.append(
-                (
-                    own_half(head, query),
-                    own_half(head, grad_o),
-                    far.astype(BF16),
-                    near.astype(BF16),
-                    far_ds,
-                    near_ds,
-                )
-            )
-        own_q, own_do, far, near, far_ds, near_ds = (
-            jnp.concatenate(part, 0) for part in zip(*kept)
-        )
-        dkx[pair, own_keys] += t_dot(far_ds, own_q)
-        dvx[pair, own_keys] += t_dot(far, own_do)
-        dkg[pair, own_rows] += t_dot(near_ds, own_q)
-        dvg[pair, own_rows] += t_dot(near, own_do)
-        glob_dq = jnp.where(low_lanes, outs[0], outs[1]) * scale
-        for at, grad in enumerate((glob_dq, dkg[pair], dvg[pair])):
-            glob_send[:, pair, :, at * PAIR : (at + 1) * PAIR] = grad.astype(BF16).reshape(
-                seq_count, quarter, PAIR
-            )
-        for copy in glob_copies(pair):
-            copy.start()
+        close_pair(pair - 1)
 
     @pl.when(number == 2 * pairs - 1)
     def _():
-        for direction in range(2):
-
-            @pl.when(gets_from[direction])
-            def _(direction=direction):
-                halo_copy(direction).wait_recv()
-
-            @pl.when(jnp.logical_not(gets_from[direction]))
-            def _(direction=direction):
-                halo_recv[direction] = jnp.zeros_like(halo_recv[direction])
-
+        if reduces:
+            run_plan(2 * pairs)
+        close_pair(pairs - 1)
         for at in range(pairs):
-            lanes = slice(at * PAIR, (at + 1) * PAIR)
-            for kind, (total, out) in enumerate(((dkx, dk_ref), (dvx, dv_ref))):
-                first, last = HALO + REACH, HALO + block - REACH
-                out[:REACH, lanes] = (
-                    total[at, HALO:first] + halo_recv[1, kind, at].astype(F32)
-                ).astype(BF16)
-                out[REACH : block - REACH, lanes] = total[at, first:last].astype(BF16)
-                out[block - REACH : block, lanes] = (
-                    total[at, last : HALO + block] + halo_recv[0, kind, at].astype(F32)
-                ).astype(BF16)
-        for at in range(pairs):
-            lanes = slice(at * PAIR, (at + 1) * PAIR)
-            total = glob_send[seq_index, at].astype(F32)
-            for step, copy in enumerate(glob_copies(at)):
-                copy.wait_recv()
-                total += glob_recv[step, at].astype(F32)
-            for kind, out in enumerate((dq_ref, dk_ref, dv_ref)):
-                out[block:, lanes] = total[:, kind * PAIR : (kind + 1) * PAIR].astype(BF16)
-        for at in range(pairs):
-            for copy in glob_copies(at):
-                copy.wait_send()
-        for copy in every_copies():
-            copy.wait_send()
-        for direction in range(2):
-
-            @pl.when(sends_to[direction])
-            def _(direction=direction):
-                halo_copy(direction).wait_send()
+            for kind in range(2):
+                for copy in glob_copies(kind, at):
+                    copy.wait_send()
+            for direction in range(2):
+
+                @pl.when(sends_to[direction])
+                def _(direction=direction, at=at):
+                    halo_copy(direction, at).wait_send()
 
         if reduces:
             reducer.finish(early_ref)
 
 
-def attend_back(sizes, doc_len, table, q, kx, vx, kg, vg, o, do, l, doq, ldq, pieces=None):
-    block, count, quarter, seq_count, pairs, early_rows = sizes
+def attend_back(sizes, doc_len, table, q, kx, vx, kg, vg, o, do, l, dog, ldg, pieces=None):
+    block, count, quarter, seq_count, pairs = sizes
     width = q.shape[1]
+    early_rows = 0 if pieces is None else pieces.shape[-2]
     ext = block + 2 * HALO
     cols = lambda rows: pl.BlockSpec((rows, PAIR), lambda i: (0, lax.rem(i, pairs)))
     whole = pl.BlockSpec(memory_space=pltpu.VMEM)
@@ -959,7 +1307,7 @@
         cols(block),
         cols(block),
         whole,
-        whole,
+        cols(GP),
         whole,
     ]
     rows = block + quarter
@@ -970,27 +1318,25 @@
         pltpu.VMEM((pairs, ext, PAIR), F32),
         pltpu.VMEM((pairs, GP, PAIR), F32),
         pltpu.VMEM((pairs, GP, PAIR), F32),
-        pltpu.VMEM((seq_count, pairs, quarter, 3 * PAIR), BF16),
-        pltpu.VMEM((others, pairs, quarter, 3 * PAIR), BF16),
-        pltpu.VMEM((2, 2, pairs, REACH, PAIR), BF16),
-        pltpu.VMEM((2, 2, pairs, REACH, PAIR), BF16),
-        pltpu.VMEM((seq_count, quarter, width), BF16),
-        pltpu.VMEM((seq_count, quarter, PAIR), F32),
-        pltpu.SemaphoreType.DMA((2, others)),
-        pltpu.SemaphoreType.DMA((2, others)),
-        pltpu.SemaphoreType.DMA((others, pairs)),
-        pltpu.SemaphoreType.DMA((others, pairs)),
-        pltpu.SemaphoreType.DMA((2,)),
-        pltpu.SemaphoreType.DMA((2,)),
+        pltpu.VMEM((seq_count, pairs, quarter, PAIR), BF16),
+        pltpu.VMEM((others, pairs, quarter, PAIR), BF16),
+        pltpu.VMEM((seq_count, pairs, quarter, 2 * PAIR), BF16),
+        pltpu.VMEM((others, pairs, quarter, 2 * PAIR), BF16),
+        pltpu.VMEM((2, pairs, 2, REACH, PAIR), BF16),
+        pltpu.VMEM((2, pairs, 2, REACH, PAIR), BF16),
+        pltpu.SemaphoreType.DMA((2, others, pairs)),
+        pltpu.SemaphoreType.DMA((2, others, pairs)),
+        pltpu.SemaphoreType.DMA((2, pairs)),
+        pltpu.SemaphoreType.DMA((2, pairs)),
     ]
-    args = [doc_len, table, q, kx, vx, kg, vg, o, do, l, doq, ldq]
+    args = [doc_len, table, q, kx, vx, kg, vg, o, do, l, dog, ldg]
     if early_rows:
         in_specs.append(pl.BlockSpec(memory_space=pl.ANY))
         outs.append(shape((early_rows, width), F32))
         scratch += Reducer.scratch(early_rows, width)
         args.append(pieces)
     return pl.pallas_call(
-        functools.partial(back_kernel, sizes),
+        functools.partial(back_kernel, sizes, early_rows),
         grid=(2 * pairs,),
         in_specs=in_specs,
         out_specs=[whole] * len(outs),
@@ -1049,7 +1395,6 @@
     labels = 2 * R + 1
     quarter = GP // seq_count
     sizes = Sizes(block, count, quarter, seq_count, pairs)
-    row_valid = (seq_index * block + jnp.arange(block, dtype=jnp.int32)) < lengths[0]
     table = jnp.pad(
         rel_table.T,
         ((0, 0), (HALO - R, WINDOW - labels - HALO + R)),
@@ -1059,7 +1404,7 @@
     glob_x = jnp.pad(global_input[0], ((0, GP - count), (0, 0)))
     glob_dy = jnp.pad(global_cotangent[0], ((0, GP - count), (0, 0)))
     own_glob = lambda a: lax.dynamic_slice_in_dim(a, seq_index * quarter, quarter, 0)
-    own_x = jnp.concatenate([long_input[0], own_glob(glob_x)], 0).astype(F32)
+    row = lambda vector: vector.reshape(1, -1)
     queries, kx, vx, kg, vg, attn_low, long_l, glob_l = attend(
         sizes,
         lengths,
@@ -1069,62 +1414,31 @@
         w_query,
         w_key,
         w_value,
-        b_query[None],
-        b_value[None],
-        norm1_gain[None],
-        norm1_shift[None],
+        row(b_query),
+        row(b_value),
+        row(norm1_gain),
+        row(norm1_shift),
     )
 
-    residual_mid = own_x + matmul(attn_low, w_out) + b_out
-    normed_two, hat_two, inv_two = norm_forward(residual_mid, norm2_gain, norm2_shift)
-    normed_two_low = normed_two.astype(BF16)
-    hidden_pre = matmul(normed_two_low, w_inner) + b_inner
-    activated, gelu_back = jax.vjp(smooth_gate, hidden_pre)
-    activated_low = activated.astype(BF16)
-    result = residual_mid + matmul(activated_low, w_outer) + b_outer
-    long_result = jnp.where(row_valid[:, None], result[:block], 0.0).astype(BF16)
-    grad_y_low = jnp.concatenate(
-        [
-            jnp.where(row_valid[:, None], long_cotangent[0], jnp.zeros_like(long_cotangent[0])),
-            own_glob(glob_dy),
-        ],
-        0,
-    )
-    grad_y = grad_y_low.astype(F32)
-    grad_b_outer = jnp.sum(grad_y, 0)
-    grad_w_outer = rows_dot(activated_low, grad_y_low)
-    (grad_hidden,) = gelu_back(back_dot(grad_y_low, w_outer))
-    grad_b_inner = jnp.sum(grad_hidden, 0)
-    hidden_low = grad_hidden.astype(BF16)
-    grad_w_inner = rows_dot(normed_two_low, hidden_low)
-    grad_from_two, grad_gain_two, grad_shift_two = norm_backward(
-        back_dot(hidden_low, w_inner), hat_two, inv_two, norm2_gain
-    )
-    grad_mid = grad_y + grad_from_two
-    grad_b_out = jnp.sum(grad_mid, 0)
-    grad_mid_low = grad_mid.astype(BF16)
-    grad_w_out = rows_dot(attn_low, grad_mid_low)
-    grad_attn = back_dot(grad_mid_low, w_out).astype(BF16)
-
-    glob_do = grad_attn[block:]
-    glob_o = attn_low[block:].astype(F32)
-    glob_delta = jnp.sum((glob_do.astype(F32) * glob_o).reshape(quarter, heads, HD), -1)
-    stats = jnp.concatenate(
-        [glob_l[:, :HD], jnp.pad(glob_delta, ((0, 0), (0, HD - heads)))], 1
-    )
-    devices = data_count * seq_count
-    piece = width // devices
-    by_device = lambda grad: grad.reshape(devices, -1, width)
-
-    def wide(grad):
-        blocks = grad.reshape(devices, piece, -1, width)
-        return blocks.transpose(0, 2, 1, 3).reshape(devices, -1, width)
-
-    inner_rows = wide(grad_w_inner).shape[1]
-    early_parts = jnp.concatenate([by_device(grad_w_outer), wide(grad_w_inner)], 1)
     planned = has_plan()
-    sizes = BackSizes(
-        block, count, quarter, seq_count, pairs, early_parts.shape[1] if planned else 0
+    long_result, glob_out, grad_mid, grad_attn, every_do, every_ld, *gradients = feed_forward(
+        sizes,
+        planned,
+        lengths,
+        attn_low,
+        long_input[0],
+        glob_x,
+        long_cotangent[0],
+        glob_dy,
+        glob_l,
+        w_out,
+        row(b_out),
+        row(norm2_gain),
+        row(norm2_shift),
+        w_inner,
+        row(b_inner),
+        w_outer,
+        row(b_outer),
     )
     query_low, key_low, value_low, dtab, *early = attend_back(
         sizes,
@@ -1135,14 +1449,22 @@
         vx,
         kg,
         vg,
-        attn_low[:block],
-        grad_attn[:block],
+        attn_low,
+        grad_attn,
         long_l,
-        glob_do,
-        stats,
-        *([by_core(early_parts)] if planned else []),
+        every_do,
+        every_ld,
+        *(gradients[:1] if planned else []),
     )
-    early = early[0] if planned else scattered(early_parts)
+    devices = data_count * seq_count
+    piece = width // devices
+    by_device = lambda grad: grad.reshape(devices, -1, width)
+    own_part = lambda vector: lax.dynamic_slice_in_dim(
+        vector,
+        (lax.axis_index("dp") * seq_count + seq_index) * (vector.shape[0] // devices),
+        vector.shape[0] // devices,
+    )
+    own_x = jnp.concatenate([long_input[0], own_glob(glob_x)], 0).astype(F32)
     own_normed, hat_one, inv_one = norm_forward(own_x, norm1_gain, norm1_shift)
     own_normed = own_normed.astype(BF16)
     grad_b_query = jnp.sum(query_low.astype(F32), 0)
@@ -1158,43 +1480,39 @@
     )
     grad_x = grad_mid + grad_from_one
 
-    g_outer = early[:-inner_rows]
-    g_inner = early[-inner_rows:].reshape(-1, piece, width).transpose(1, 0, 2)
-    vectors = (
-        grad_b_query,
-        grad_b_value,
-        grad_b_out,
-        grad_b_inner,
-        grad_b_outer,
-        grad_gain_one,
-        grad_shift_one,
-        grad_gain_two,
-        grad_shift_two,
-    )
-    small = jnp.concatenate([v.reshape(devices, -1) for v in vectors], 1)
-    small = jnp.pad(small, ((0, 0), (0, width - small.shape[1])))
-    small = jnp.pad(small[:, None], ((0, 0), (0, 15), (0, 0)))
-    late_parts = jnp.concatenate(
-        [by_device(g) for g in (grad_w_query, grad_w_key, grad_w_value, grad_w_out)] + [small], 1
-    )
+    vectors = jnp.stack([grad_b_query, grad_b_value, grad_gain_one, grad_shift_one])
+    grads = (grad_w_query, grad_w_key, grad_w_value)
     table_part = dtab.reshape(heads, WINDOW)
     if planned:
-        late, table_total = reduce_late(by_core(late_parts), table_part)
+        g_outer, early = gradients[1], early[0]
+        g_inner = early[: 4 * piece].reshape(4, piece, width).transpose(1, 0, 2)
+        g_inner = g_inner.reshape(piece, -1)
+        g_out, early_vectors = early[4 * piece : 5 * piece], early[5 * piece :]
+        extra = jnp.broadcast_to(jnp.pad(vectors, ((0, 4), (0, 0))), (devices, 8, width))
+        late, table_total = reduce_late(
+            by_core(jnp.concatenate([by_device(g) for g in grads] + [extra], 1)), table_part
+        )
+        g_query, g_key, g_value = (late[i * piece : (i + 1) * piece] for i in range(3))
+        vectors = late[3 * piece :]
     else:
-        late, table_total = scattered(late_parts), lax.psum(table_part, ("dp", "seq"))
+        g_outer, g_inner, g_out, early_vectors = gradients
+        g_outer, g_inner, g_out, g_query, g_key, g_value = (
+            lax.psum_scatter(g.astype(BF16), ("dp", "seq"), scatter_dimension=0, tiled=True).astype(
+                F32
+            )
+            for g in (g_outer, g_inner, g_out) + grads
+        )
+        early_vectors, vectors, table_total = lax.psum(
+            (early_vectors, vectors, table_part), ("dp", "seq")
+        )
+    g_b_query, g_b_value, g_g1, g_s1 = (own_part(vectors[i]) for i in range(4))
+    g_b_out, g_b_outer, g_g2, g_s2 = (own_part(early_vectors[i]) for i in range(4))
+    g_b_inner = own_part(early_vectors[4:].reshape(-1))
     table_total = table_total[:, HALO - R : HALO - R + labels].T
-    pieces, at = [], 0
-    for vector in vectors:
-        length = vector.shape[0] // devices
-        pieces.append(late[4 * piece, at : at + length])
-        at += length
-    g_b_query, g_b_value, g_b_out, g_b_inner, g_b_outer, g_g1, g_s1, g_g2, g_s2 = pieces
-    g_query, g_key, g_value, g_out = (late[i * piece : (i + 1) * piece] for i in range(4))
-    glob_out = lax.all_gather(result[block:].astype(BF16), "seq", axis=0, tiled=True)[:count]
     glob_grad = lax.all_gather(grad_x[block:], "seq", axis=0, tiled=True)[:count]
     return (
         long_result[None],
-        glob_out[None],
+        glob_out[:count][None],
         grad_x[:block][None],
         glob_grad[None],
         g_query,
@@ -1204,7 +1522,7 @@
         g_b_value,
         g_out,
         g_b_out,
-        g_inner.reshape(piece, -1),
+        g_inner,
         g_b_inner,
         g_outer,
         g_b_outer,

time: 281 us -> 260 us (0.925); the launches traced: 276 us -> 260 us
  Pallas kernels: 140 us -> 203 us
  matrix products: 61.1 us -> 14.2 us
  other arithmetic: 18.5 us -> 5.04 us
  local copies, waits for them, and re-layouts: 38.2 us -> 27.7 us
  blocking collectives: 15.8 us -> 8.61 us
    pallas_call x1 -> x2, Pallas kernels: 71.9 us -> 144 us  [the longest x1 76.4 us: attend_back(): pl.pallas_call(functools.partial(back_kernel, sizes, early_rows), grid=(2...]
    dot_general x6 -> x3, matrix products: 26.4 us -> 4.22 us  [rows_dot(): return jnp.einsum('rd,re->de', left, right, preferred_element_type=F32)]
    dot_general x6 -> x3, matrix products: 25 us -> 9.97 us  [back_dot(): lax.dot_general(left, right, (((1,), (1,)), ((), ())), preferred_element_...]
    dot_general x3 -> x0, matrix products: 9.67 us -> none  [matmul(): return jnp.dot(left, right, preferred_element_type=F32)]
    pallas_call x1, Pallas kernels: 38.3 us -> 28.9 us  [reduce_late(): pl.pallas_call(functools.partial(late_kernel, rows), in_specs=[pl.BlockSp...]
    all_gather x1 -> x0, blocking collectives: 6.91 us -> none  [on_device(): lax.all_gather(result[block:].astype(BF16), 'seq', axis=0, tiled=True)]
    reshape x13 -> x10, local copies, waits for them, and re-layouts: 14.7 us -> 8.13 us  [the longest x8 7.39 us: on_device(): row = lambda vector: vector.reshape(1, -1)]
    reduce_sum x6 -> x0, other arithmetic: 5.86 us -> none  [the longest x3 2.28 us: on_device(): grad_b_outer = jnp.sum(grad_y, 0)]
where the time goes in v1:
time: 260 us
  Pallas kernels  203 us (78%)
  local copies, waits for them, and re-layouts  27.7 us (11%)
  matrix products  14.2 us (5%)
  blocking collectives  8.61 us (3%)
  other arithmetic  5.04 us (2%)
    pallas_call x1, Pallas kernels, attend_back(): pl.pallas_call(functools.partial(back_kernel, sizes, early_rows), grid=(2...  76.4 us
    pallas_call x1, Pallas kernels, feed_forward(): pl.pallas_call(functools.partial(ffn_kernel, sizes, planned), grid=(4,),...  67.9 us
    pallas_call x1, Pallas kernels, attend(): pl.pallas_call(functools.partial(attend_kernel, sizes), in_specs=[pl.Bloc...  29.3 us
    pallas_call x1, Pallas kernels, reduce_late(): pl.pallas_call(functools.partial(late_kernel, rows), in_specs=[pl.BlockSp...  28.9 us
    dot_general x3, matrix products, back_dot(): lax.dot_general(left, right, (((1,), (1,)), ((), ())), preferred_element_...  9.97 us
    all_gather x1, blocking collectives, on_device(): lax.all_gather(grad_x[block:], 'seq', axis=0, tiled=True)[:count]  8.61 us
    reshape x8, local copies, waits for them, and re-layouts, on_device(): row = lambda vector: vector.reshape(1, -1)  7.39 us
    unnamed x53, local copies, waits for them, and re-layouts  5.85 us

profile of v1, /device:TPU:0, one launch (start us, length us, event | category | flops | bytes accessed | tf_op | source)
XLA Modules:
  0.0 259.9 jit_solution(2967716676953626475)
XLA Ops:
  0.7 1.8 pad.16.glob_ref
  3.1 0.8 pad.15
  4.5 1.3 reshape.127.bq_ref
  5.8 1.3 reshape.128.bv_ref
  7.0 1.3 reshape.129.gain_ref
  8.3 1.3 reshape.130.shift_ref
  9.6 29.3 %attend.1 = (bf16[768,768]{1,0:T(8,128)(2,1)}, bf16[768,768]{1,0:T(8,128)(2,1)}, bf16[768,768]{1,0:T(8,128)(2,1)}, bf16[256,768]{1,0:T(8,128)(2,1)}, bf16[256,76...) custom-call(s32[1]{0:T(128)S(6)} %copy.57.len_ref, ...), custom_call_target="tpu_custom_call" | custom-call | tf_op jit(solution)/shard_map/attend/pallas_call | solution.py:355
  42.0 67.9 %feed_forward.1 = (bf16[512,768]{1,0:T(8,128)(2,1)}, bf16[256,768]{1,0:T(8,128)(2,1)}, f32[576,768]{1,0:T(8,128)}, bf16[576,768]{1,0:T(8,128)(2,1)}, bf16[256,76...) custom-call(s32[1]{0:T(128)S(6)} %copy.57.len_ref, ...), custom_call_target="tpu_custom_call" | custom-call | tf_op jit(solution)/shard_map/feed_forward/pallas_call | solution.py:1010
  109.9 76.4 %attend_back.1 = (bf16[576,768]{1,0:T(8,128)(2,1)}, bf16[576,768]{1,0:T(8,128)(2,1)}, bf16[576,768]{1,0:T(8,128)(2,1)}, f32[6,2,512]{2,1,0:T(2,128)}, f32[128,768]{1,0:T(8,128)}) custom-call(s32[1]{0:T(128)S(6)} %copy.57.len_ref, f32[6,2,512]{2,1,0:T(2,128)} %reshape.126.tab_ref, bf16[768,768]{1,0:T(8,128)(2,1)} %get-tuple-element.48.q_ref, ...), custom_call_target="tpu_custom_call" | custom-call | tf_op jit(solution)/shard_map/attend_back/pallas_call | solution.py:1338
  186.4 0.9 fusion.26
  188.5 1.7 convert_reduce_fusion.1
  190.8 3.4 %fusion.29 = f32[576,768]{1,0:T(8,128)} fusion(bf16[576,768]{1,0:T(8,128)(2,1)} %get-tuple-element.58, bf16[768,768]{1,0:T(8,128)(2,1)S(1)} %copy-done.4), kind=kOutput, calls=%fused_computation.58 | convolution fusion | flops 679477248 | bytes 3833856 | tf_op jit(solution)/shard_map/dot_general | solution.py:1361
  194.2 2.1 fusion.30
  197.5 4.4 %fusion.12 = (bf16[768]{0:T(1024)(128)(2,1)S(1)}, f32[576]{0:T(1024)}, f32[576]{0:T(1024)}, bf16[768]{0:T(1024)(128)(2,1)S(1)}, f32[576,768]{1,0:T(8,128)S(1)}) fusion(f32[576]{0:T(1024)S(1)} %add_rsqrt_fusion, f32[576]{0:T(1024)S(1)} %broadcast_multiply_fusion.2, bf16[64,768]{1,0:T(8,128)(2,1)S(1)} %constant_dynamic-slice_fusion.8, ...), kind=kOutput, calls=%fused_computation.15 | convolution fusion | flops 686110080 | bytes 8272896 | tf_op jit(solution)/shard_map/dot_general | solution.py:1361
  202.1 1.4 convolution_convert_fusion.2
  203.5 1.4 convolution_convert_fusion.1
  204.9 1.4 convolution_convert_fusion
  206.3 2.0 maximum_bitcast_fusion.pieces_ref
  208.4 2.1 copy-done
  210.5 28.9 %reduce_late.1 = (f32[80,768]{1,0:T(8,128)S(1)}, f32[12,512]{1,0:T(8,128)S(1)}) custom-call(bf16[2,4,2,2,80,768]{5,4,3,2,1,0:T(8,128)(2,1)S(1)} %copy-done, f32[12,512]{1,0:T(8,128)S(1)} %reshape.136.table_ref), custom_call_target="tpu_custom_call" | custom-call | tf_op jit(solution)/shard_map/reduce_late/pallas_call | solution.py:669
  243.8 8.6 %all_gather.3 = f32[256,768]{1,0:T(8,128)S(1)} all-gather(f32[64,768]{1,0:T(8,128)S(1)} %slice.88), channel_id=1, replica_groups=mesh['dp'=8,'seq'=4] {'seq'}, dimensions={0}, use_global_device_ids=true | all-gather | bytes 983040 | tf_op jit(solution)/shard_map/all_gather | solution.py:1512
  252.5 1.6 copy.47
  254.1 1.2 slice_bitcast_fusion
  258.1 0.9 copy.58
  (88 shorter events, 14.7 us)
Async XLA Ops:
  9.6 29.3 %copy-start.10 = (bf16[1,230,768]{2,1,0:T(8,128)(2,1)S(1)}, bf16[1,230,768]{2,1,0:T(8,128)(2,1)}, u32[]{:S(2)}) copy-start(bf16[1,230,768]{2,1,0:T(8,128)(2,1)} %param.41) | copy-start | bytes 1059844
  9.6 30.1 %copy-start.16 = (f32[768]{0:T(1024)S(1)}, f32[768]{0:T(1024)}, u32[]{:S(2)}) copy-start(f32[768]{0:T(1024)} %param.30) | copy-start | bytes 9220
  9.6 30.7 %copy-start.17 = (f32[768]{0:T(1024)S(1)}, f32[768]{0:T(1024)}, u32[]{:S(2)}) copy-start(f32[768]{0:T(1024)} %param.37) | copy-start | bytes 9220
  9.6 31.3 %copy-start.18 = (f32[768]{0:T(1024)S(1)}, f32[768]{0:T(1024)}, u32[]{:S(2)}) copy-start(f32[768]{0:T(1024)} %param.38) | copy-start | bytes 9220
  9.6 31.9 %copy-start.19 = (f32[768]{0:T(1024)S(1)}, f32[768]{0:T(1024)}, u32[]{:S(2)}) copy-start(f32[768]{0:T(1024)} %param.34) | copy-start | bytes 9220
  186.4 4.4 %copy-start.4 = (bf16[768,768]{1,0:T(8,128)(2,1)S(1)}, bf16[768,768]{1,0:T(8,128)(2,1)}, u32[]{:S(2)}) copy-start(bf16[768,768]{1,0:T(8,128)(2,1)} %wq_ref.1) | copy-start | bytes 3538948
  190.8 3.4 %copy-start.5 = (bf16[768,768]{1,0:T(8,128)(2,1)S(1)}, bf16[768,768]{1,0:T(8,128)(2,1)}, u32[]{:S(2)}) copy-start(bf16[768,768]{1,0:T(8,128)(2,1)} %wk_ref.1) | copy-start | bytes 3538948
  190.8 3.4 %copy-start.23 = (bf16[576,768]{1,0:T(8,128)(2,1)S(1)}, bf16[576,768]{1,0:T(8,128)(2,1)}, u32[]{:S(2)}) copy-start(bf16[576,768]{1,0:T(8,128)(2,1)} %get-tuple-element.59) | copy-start | bytes 2654212
  194.2 2.1 copy-start.3
  194.2 2.2 copy-start.1
  196.3 1.2 copy-start.14
  197.5 4.5 %copy-start.15 = (bf16[1,768]{1,0:T(2,128)(2,1)S(1)}, bf16[1,768]{1,0:T(2,128)(2,1)}, u32[]{:S(2)}) copy-start(bf16[1,768]{1,0:T(2,128)(2,1)} %stack.16) | copy-start | bytes 4612
  197.5 4.5 %copy-start.7 = (bf16[576,768]{1,0:T(8,128)(2,1)S(1)}, bf16[576,768]{1,0:T(8,128)(2,1)}, u32[]{:S(2)}) copy-start(bf16[576,768]{1,0:T(8,128)(2,1)} %get-tuple-element.58) | copy-start | bytes 2654212
  197.5 4.5 %copy-start.20 = (f32[768]{0:T(1024)S(1)}, f32[768]{0:T(1024)}, u32[]{:S(2)}) copy-start(f32[768]{0:T(1024)} %param.36) | copy-start | bytes 9220
  202.1 1.4 copy-start.24
  206.3 2.0 copy-start.13
  208.4 2.1 copy-start
  210.5 32.7 %copy-start.21 = (f32[576]{0:T(1024)S(1)}, f32[576]{0:T(1024)}, u32[]{:S(2)}) copy-start(f32[576]{0:T(1024)} %get-tuple-element.107) | copy-start | bytes 6916
  210.5 32.7 %copy-start.22 = (f32[576]{0:T(1024)S(1)}, f32[576]{0:T(1024)}, u32[]{:S(2)}) copy-start(f32[576]{0:T(1024)} %get-tuple-element.108) | copy-start | bytes 6916
  210.5 32.7 %copy-start.2 = (f32[576,768]{1,0:T(8,128)S(1)}, f32[576,768]{1,0:T(8,128)}, u32[]{:S(2)}) copy-start(f32[576,768]{1,0:T(8,128)} %get-tuple-element.47) | copy-start | bytes 5308420
  254.1 1.3 copy-start.9
  254.1 3.3 %copy-start.11 = (bf16[256,768]{1,0:T(8,128)(2,1)S(1)}, bf16[256,768]{1,0:T(8,128)(2,1)}, u32[]{:S(2)}) copy-start(bf16[256,768]{1,0:T(8,128)(2,1)} %get-tuple-element.46) | copy-start | bytes 1179652
  255.3 2.8 %copy-start.8 = (bf16[512,768]{1,0:T(8,128)(2,1)S(1)}, bf16[512,768]{1,0:T(8,128)(2,1)}, u32[]{:S(2)}) copy-start(bf16[512,768]{1,0:T(8,128)(2,1)} %get-tuple-element.45) | copy-start | bytes 2359300
  255.3 3.7 %copy-start.12 = (f32[96,768]{1,0:T(8,128)S(1)}, f32[96,768]{1,0:T(8,128)}, u32[]{:S(2)}) copy-start(f32[96,768]{1,0:T(8,128)} %get-tuple-element.163) | copy-start | bytes 884740
  (1 other events, 1.2 us)
